TPU v7x, 256 devices: a whole 4x4x8 slice. The times are simulated.
256 devices in a mesh: dp: 8 (over z_lo, core), seq: 32 (over y, x, z_hi).
Axes of the slice: x: 4, y: 4, z: 8 (z_hi: 2, z_lo: 4; z = z_hi * 4 + z_lo), core: 2. Of those that a mesh axis runs over, the one named last changes fastest.
Arguments:
- first_input: bfloat16 [8, 16384, 128], P('dp', 'seq'), may hold values from -6 to 6
- value_input: bfloat16 [8, 16384, 128], P('dp', 'seq'), may hold values from -6 to 6
- gate_input: bfloat16 [8, 16384, 128], P('dp', 'seq'), may hold values from -6 to 6
- cotangent: bfloat16 [8, 16384, 128], P('dp', 'seq'), may hold values from -6 to 6
- filter_taps: float32 [16384, 128], P('seq'), may hold values from -4 to 4
- skip_weight: float32 [128], replicated, may hold values from -4 to 4
Outputs:
- layer_output: bfloat16 [8, 16384, 128], P('dp', 'seq')
- filter_grad: float32 [16384, 128], P('seq')
All inputs are finite; a program needn't handle non-finite values.
Results may differ from a plain program's by a relative error of at most 0.001.
Values sent between devices are 32-bit elements; how exact they have to be, the bound alone decides.
A program may use at most 64 MiB of HBM per device.

v0:
```python
import functools
import math

import jax
import jax.numpy as jnp
from jax import lax
from jax.sharding import PartitionSpec as P


def angles(numer, period):
    return 2.0 * math.pi / period * (numer % period).astype(jnp.float32)


def rotate(real_part, imag_part, phase, direction):
    cosine = jnp.cos(phase)
    sine = direction * jnp.sin(phase)
    return (real_part * cosine - imag_part * sine, real_part * sine + imag_part * cosine)


def local_transform(real_part, imag_part, direction):
    count, length = real_part.shape
    outer = 1 << (length.bit_length() - 1) // 2
    inner = length // outer
    real_cube = real_part.reshape(count, outer, inner)
    imag_cube = imag_part.reshape(count, outer, inner)
    outer_idx = lax.iota(jnp.int32, outer)
    inner_idx = lax.iota(jnp.int32, inner)
    first_phase = angles(outer_idx[:, None] * outer_idx[None, :], outer)
    first_cos = jnp.cos(first_phase)
    first_sin = direction * jnp.sin(first_phase)
    mix = functools.partial(
        jnp.einsum, precision=lax.Precision.HIGHEST, preferred_element_type=jnp.float32
    )
    section_real = mix("kp,cpq->ckq", first_cos, real_cube) - mix(
        "kp,cpq->ckq", first_sin, imag_cube
    )
    section_imag = mix("kp,cpq->ckq", first_cos, imag_cube) + mix(
        "kp,cpq->ckq", first_sin, real_cube
    )
    twiddle = angles(outer_idx[:, None] * inner_idx[None, :], length)
    section_real, section_imag = rotate(section_real, section_imag, twiddle, direction)
    second_phase = angles(inner_idx[:, None] * inner_idx[None, :], inner)
    second_cos = jnp.cos(second_phase)
    second_sin = direction * jnp.sin(second_phase)
    final_real = mix("ckq,jq->ckj", section_real, second_cos) - mix(
        "ckq,jq->ckj", section_imag, second_sin
    )
    final_imag = mix("ckq,jq->ckj", section_imag, second_cos) + mix(
        "ckq,jq->ckj", section_real, second_sin
    )
    final_real = jnp.transpose(final_real, (0, 2, 1)).reshape(count, length)
    final_imag = jnp.transpose(final_imag, (0, 2, 1)).reshape(count, length)
    return (final_real, final_imag)


def channel_layout(gated, weighted, filter_taps, gate_input, skip_weight):
    batch_local = gated.shape[0]
    moved_gated, moved_weighted, moved_taps = (
        lax.all_to_all(gated, "seq", split_axis=2, concat_axis=1, tiled=True),
        lax.all_to_all(weighted, "seq", split_axis=2, concat_axis=1, tiled=True),
        lax.all_to_all(filter_taps[None], "seq", split_axis=2, concat_axis=1, tiled=True),
    )
    length = moved_gated.shape[1]
    narrow = moved_gated.shape[2]
    spread = batch_local * narrow
    gated_rows = jnp.transpose(moved_gated, (0, 2, 1)).reshape(spread, length)
    weighted_rows = jnp.transpose(moved_weighted, (0, 2, 1)).reshape(spread, length)
    taps_rows = jnp.transpose(moved_taps[0], (1, 0))
    rows_all = jnp.concatenate([gated_rows, taps_rows, weighted_rows], axis=0)
    count = rows_all.shape[0]
    twist = angles(lax.iota(jnp.int32, length), 2 * length)[None, :]
    cos_twist = jnp.cos(twist)
    sin_twist = jnp.sin(twist)
    real_in = jnp.concatenate([rows_all, rows_all * cos_twist], axis=0)
    imag_in = jnp.concatenate([jnp.zeros_like(rows_all), -rows_all * sin_twist], axis=0)
    spec_real, spec_imag = local_transform(real_in, imag_in, -1.0)
    spec_real = spec_real.reshape(2, count, length)
    spec_imag = spec_imag.reshape(2, count, length)
    gated_real = spec_real[:, :spread].reshape(2, batch_local, narrow, length)
    gated_imag = spec_imag[:, :spread].reshape(2, batch_local, narrow, length)
    taps_real = spec_real[:, spread : spread + narrow][:, None]
    taps_imag = spec_imag[:, spread : spread + narrow][:, None]
    source_real = spec_real[:, spread + narrow :].reshape(2, batch_local, narrow, length)
    source_imag = spec_imag[:, spread + narrow :].reshape(2, batch_local, narrow, length)
    conv_real = (gated_real * taps_real - gated_imag * taps_imag).reshape(2, spread, length)
    conv_imag = (gated_real * taps_imag + gated_imag * taps_real).reshape(2, spread, length)
    grad_real = jnp.sum(source_real * gated_real + source_imag * gated_imag, axis=1)
    grad_imag = jnp.sum(source_imag * gated_real - source_real * gated_imag, axis=1)
    back_real = jnp.concatenate([conv_real, grad_real], axis=1).reshape(-1, length)
    back_imag = jnp.concatenate([conv_imag, grad_imag], axis=1).reshape(-1, length)
    back_real, back_imag = local_transform(back_real, back_imag, 1.0)
    back_real = back_real.reshape(2, -1, length)
    back_imag = back_imag.reshape(2, -1, length)
    joined = (back_real[0] + back_real[1] * cos_twist - back_imag[1] * sin_twist) / (2.0 * length)
    convolved = jnp.transpose(joined[:spread].reshape(batch_local, narrow, length), (0, 2, 1))
    grad_time = lax.psum(jnp.transpose(joined[spread:], (1, 0)), "dp")
    convolved, grad_back = (
        lax.all_to_all(convolved, "seq", split_axis=1, concat_axis=2, tiled=True),
        lax.all_to_all(grad_time[None], "seq", split_axis=1, concat_axis=2, tiled=True),
    )
    layer_output = (gate_input.astype(jnp.float32) * (convolved + skip_weight * gated)).astype(
        jnp.bfloat16
    )
    scale = 1.0 / math.sqrt(batch_local * lax.axis_size("dp") * length)
    return (layer_output, grad_back[0] * scale)


def shards(first_input, value_input, gate_input, cotangent, filter_taps, skip_weight):
    gated = first_input.astype(jnp.float32) * value_input.astype(jnp.float32)
    weighted = cotangent.astype(jnp.float32) * gate_input.astype(jnp.float32)
    return channel_layout(gated, weighted, filter_taps, gate_input, skip_weight)


def solution(mesh):
    placed = (
        P("dp", "seq", None),
        P("dp", "seq", None),
        P("dp", "seq", None),
        P("dp", "seq", None),
        P("seq", None),
        P(),
    )
    return jax.shard_map(
        shards,
        mesh=mesh,
        in_specs=placed,
        out_specs=(P("dp", "seq", None), P("seq", None)),
        check_vma=False,
    )
```

profile of v0, /device:TPU:1, one launch (start us, length us, event | category | flops | bytes accessed | tf_op | source)
XLA Modules:
  0.0 485.8 jit_solution(10669566144408117033)
XLA Ops:
  9.1 14.5 %all-to-all-start.2 = ((f32[1,512,128]{1,0,2:T(1,128)}), f32[1,512,128]{1,0,2:T(1,128)S(1)}, u32[]{:S(2)}, u32[]{:S(2)}) async-start(f32[1,512,128]{1,0,2:T(1,128)} %copy.157), calls=%async_computation.2 | async-start | bytes 524288 | tf_op jit(solution)/shard_map/all_to_all | solution.py:60
  24.4 11.8 %all-to-all-done.2 = f32[1,512,128]{1,0,2:T(1,128)S(1)} async-done(((f32[1,512,128]{1,0,2:T(1,128)}), f32[1,512,128]{1,0,2:T(1,128)S(1)}, u32[]{:S(2)}, u32[]{:S(2)}) %all-to-all-start.2) | async-done | bytes 262176 | tf_op jit(solution)/shard_map/all_to_all | solution.py:60
  36.2 3.9 all-to-all-start.1
  41.8 10.5 %all-to-all-done.1 = f32[1,512,128]{1,0,2:T(1,128)S(1)} async-done(((f32[1,512,128]{1,0,2:T(1,128)}), f32[1,512,128]{1,0,2:T(1,128)S(1)}, u32[]{:S(2)}, u32[]{:S(2)}) %all-to-all-start.1) | async-done | bytes 262176 | tf_op jit(solution)/shard_map/all_to_all | solution.py:61
  52.3 4.2 all-to-all-start
  59.7 8.6 %all-to-all-done = f32[1,512,128]{1,0,2:T(1,128)S(1)} async-done(((f32[1,512,128]{1,0,2:T(1,128)}), f32[1,512,128]{1,0,2:T(1,128)S(1)}, u32[]{:S(2)}, u32[]{:S(2)}) %all-to-all-start) | async-done | bytes 262176 | tf_op jit(solution)/shard_map/all_to_all | solution.py:59
  78.5 3.4 fusion.11
  81.9 4.0 fusion.15
  85.9 4.0 add_bitcast_fusion
  96.0 5.4 %subtract_bitcast_fusion = f32[24,128,128]{1,2,0:T(8,128)} fusion(f32[24,128,128]{2,1,0:T(8,128)} %fusion.15, f32[24,128,128]{2,1,0:T(8,128)S(1)} %convolution_add_fusion, f32[24,128,128]{2,1,0:T(8,128)S(1)} %convolution_subtract_fusion, f32[128,128]{0,1:T(8,128)S(1)} %copy.169, f32[128,128]{0,1:T(8,128)S(1)} %copy.167), kind=kOutput, calls=%fused_computation.8 | convolution fusion | flops 605798400 | bytes 6422528 | tf_op jit(solution)/shard_map/ckq,jq->ckj/dot_general | solution.py:45
  101.4 3.2 copy.172
  132.8 12.0 %copy.189 = f32[1,16384,4]{2,0,1:T(1,128)} copy(f32[1,16384,4]{1,2,0:T(4,128)S(1)} %get-tuple-element.17) | data formatting | bytes 524288 | tf_op jit(solution)/shard_map/transpose | solution.py:95
  145.4 74.5 %reduce = f32[16384,4]{1,0:T(8,128)} reduce(f32[16384,1,4]{2,1,0:T(1,128)} %bitcast.179, f32[]{:T(128)} %broadcast.236), dimensions={1}, to_apply=%bitcast.163.reduce_sub_computation | reduce | bytes 524292
  219.9 9.5 %reshape.143 = f32[32,1,2048]{2,1,0:T(1,128)} reshape(f32[16384,4]{1,0:T(8,128)} %reduce) | data formatting | bytes 524288
  229.4 3.9 all-to-all-start.3
  234.0 80.0 %all-reduce.3.cloned.1.call-done = f32[1,16384,4]{1,2,0:T(4,128)} async-done(((f32[1,16384,4]{1,2,0:T(4,128)}), f32[1,16384,4]{1,2,0:T(4,128)}) %all-reduce.3.cloned.1.call-update) | async-done | bytes 262160 | tf_op jit(solution)/shard_map/psum | solution.py:96
  313.9 14.8 %copy.193 = f32[1,16384,4]{2,0,1:T(1,128)} copy(f32[1,16384,4]{1,2,0:T(4,128)} %all-reduce.3.cloned.1.call-done) | data formatting | bytes 524288 | tf_op jit(solution)/shard_map/psum | solution.py:96
  328.8 74.5 %reduce.2 = f32[16384,4]{1,0:T(8,128)} reduce(f32[16384,1,4]{2,1,0:T(1,128)} %bitcast.180, f32[]{:T(128)} %broadcast.236), dimensions={1}, to_apply=%bitcast.165.reduce_sub_computation | reduce | bytes 524292
  403.3 9.1 %reshape.145 = f32[32,1,2048]{2,1,0:T(1,128)} reshape(f32[16384,4]{1,0:T(8,128)} %reduce.2) | data formatting | bytes 524288
  412.4 11.5 %all-to-all-start.4 = ((f32[32,1,2048]{2,1,0:T(1,128)}), f32[32,1,2048]{2,1,0:T(1,128)S(1)}, u32[]{:S(2)}, u32[]{:S(2)}) async-start(f32[32,1,2048]{2,1,0:T(1,128)} %reshape.145), calls=%async_computation.4 | async-start | bytes 524288 | tf_op jit(solution)/shard_map/all_to_all | solution.py:99
  425.2 14.8 %reshape.144 = f32[16384,1,4]{2,1,0:T(1,128)} reshape(f32[32,2048]{1,0:T(8,128)S(1)} %reduce.1) | data formatting | bytes 524288
  440.0 5.3 %copy.212 = f32[1,32,512,4]{2,1,3,0:T(8,128)S(1)} copy(f32[1,32,512,4]{3,2,1,0:T(8,128)} %bitcast.181) | data formatting | bytes 524288 | tf_op jit(solution)/shard_map/all_to_all | solution.py:98
  447.7 14.8 %reshape.146 = f32[16384,1,4]{2,1,0:T(1,128)} reshape(f32[32,2048]{1,0:T(8,128)S(1)} %reduce.3) | data formatting | bytes 524288
  462.5 15.0 %copy.194 = f32[1,16384,4]{1,2,0:T(4,128)S(1)} copy(f32[1,16384,4]{2,0,1:T(1,128)} %bitcast.182) | data formatting | bytes 524288 | tf_op jit(solution)/shard_map/all_to_all | solution.py:99
  (106 shorter events, 58.0 us)
Async XLA Ops:
  7.2 16.4 %copy-start.15 = (f32[512,128]{1,0:T(8,128)S(1)}, f32[512,128]{1,0:T(8,128)}, u32[]{:S(2)}) copy-start(f32[512,128]{1,0:T(8,128)} %param.10) | copy-start | bytes 786436
  7.2 32.9 %copy-start.10 = (bf16[1,512,128]{2,1,0:T(8,128)(2,1)S(1)}, bf16[1,512,128]{2,1,0:T(8,128)(2,1)}, u32[]{:S(2)}) copy-start(bf16[1,512,128]{2,1,0:T(8,128)(2,1)} %param.7) | copy-start | bytes 393220
  7.2 32.9 %copy-start.12 = (bf16[1,512,128]{2,1,0:T(8,128)(2,1)S(1)}, bf16[1,512,128]{2,1,0:T(8,128)(2,1)}, u32[]{:S(2)}) copy-start(bf16[1,512,128]{2,1,0:T(8,128)(2,1)} %param.6) | copy-start | bytes 393220
  9.1 27.1 %all-to-all-start.2 = ((f32[1,512,128]{1,0,2:T(1,128)}), f32[1,512,128]{1,0,2:T(1,128)S(1)}, u32[]{:S(2)}, u32[]{:S(2)}) async-start(f32[1,512,128]{1,0,2:T(1,128)} %copy.157), calls=%async_computation.2 | async-start | bytes 524288 | tf_op jit(solution)/shard_map/all_to_all | solution.py:60
  36.2 16.1 %all-to-all-start.1 = ((f32[1,512,128]{1,0,2:T(1,128)}), f32[1,512,128]{1,0,2:T(1,128)S(1)}, u32[]{:S(2)}, u32[]{:S(2)}) async-start(f32[1,512,128]{1,0,2:T(1,128)} %copy.211), calls=%async_computation.1 | async-start | bytes 524288 | tf_op jit(solution)/shard_map/all_to_all | solution.py:61
  52.3 16.1 %all-to-all-start = ((f32[1,512,128]{1,0,2:T(1,128)}), f32[1,512,128]{1,0,2:T(1,128)S(1)}, u32[]{:S(2)}, u32[]{:S(2)}) async-start(f32[1,512,128]{1,0,2:T(1,128)} %copy.153), calls=%async_computation | async-start | bytes 524288 | tf_op jit(solution)/shard_map/all_to_all | solution.py:59
  57.9 10.8 %copy-start.7 = (f32[16384]{0:T(1024)}, f32[16384]{0:T(1024)S(1)}, u32[]{:S(2)}) copy-start(f32[16384]{0:T(1024)S(1)} %fusion.51) | copy-start | bytes 196612
  59.7 9.8 %copy-start.1 = (f32[4,128,128]{1,2,0:T(8,128)}, f32[4,128,128]{1,2,0:T(8,128)S(1)}, u32[]{:S(2)}) copy-start(f32[4,128,128]{1,2,0:T(8,128)S(1)} %copy.164) | copy-start | bytes 786436
  68.7 0.7 copy-start.3
  74.0 2.9 copy-start.2
  74.0 2.9 copy-start.4
  104.6 3.2 copy-start
  116.9 1.9 copy-start.6
  130.1 1.0 copy-start.5
  130.1 1.0 copy-start.8
  130.1 1.0 copy-start.14
  229.4 183.0 %all-to-all-start.3 = ((f32[32,1,2048]{2,1,0:T(1,128)}), f32[32,1,2048]{2,1,0:T(1,128)S(1)}, u32[]{:S(2)}, u32[]{:S(2)}) async-start(f32[32,1,2048]{2,1,0:T(1,128)} %reshape.143), calls=%async_computation.3 | async-start | bytes 524288 | tf_op jit(solution)/shard_map/all_to_all | solution.py:98
  233.3 80.7 %all-reduce.3.cloned.1.call-start = ((), (), s32[]{:S(2)}) async-start(), calls=%async_computation.5 | async-start | bytes 524288 | tf_op jit(solution)/shard_map/psum | solution.py:96
  412.4 34.1 %all-to-all-start.4 = ((f32[32,1,2048]{2,1,0:T(1,128)}), f32[32,1,2048]{2,1,0:T(1,128)S(1)}, u32[]{:S(2)}, u32[]{:S(2)}) async-start(f32[32,1,2048]{2,1,0:T(1,128)} %reshape.145), calls=%async_computation.4 | async-start | bytes 524288 | tf_op jit(solution)/shard_map/all_to_all | solution.py:99
  439.9 5.7 %copy-start.9 = (bf16[1,512,128]{2,1,0:T(8,128)(2,1)S(1)}, bf16[1,512,128]{2,1,0:T(8,128)(2,1)}, u32[]{:S(2)}) copy-start(bf16[1,512,128]{2,1,0:T(8,128)(2,1)} %param.8) | copy-start | bytes 393220
  439.9 5.7 %copy-start.11 = (bf16[1,512,128]{2,1,0:T(8,128)(2,1)S(1)}, bf16[1,512,128]{2,1,0:T(8,128)(2,1)}, u32[]{:S(2)}) copy-start(bf16[1,512,128]{2,1,0:T(8,128)(2,1)} %param.7) | copy-start | bytes 393220
  440.0 5.7 %copy-start.13 = (bf16[1,512,128]{2,1,0:T(8,128)(2,1)S(1)}, bf16[1,512,128]{2,1,0:T(8,128)(2,1)}, u32[]{:S(2)}) copy-start(bf16[1,512,128]{2,1,0:T(8,128)(2,1)} %param.6) | copy-start | bytes 393220
  440.0 5.7 %copy-start.16 = (f32[128]{0:T(128)S(1)}, f32[128]{0:T(128)}, u32[]{:S(2)}) copy-start(f32[128]{0:T(128)} %param.11) | copy-start | bytes 1540
Sparse Core Ops, SparseCore 0:
  237.3 76.6 all-reduce.2
where the time goes:
time: 491 us; the launch traced here: 486 us
  other arithmetic  160 us (33%)
  local copies, waits for them, and re-layouts  120 us (24%)
  waiting for transfers between devices  112 us (23%)
  matrix products  41.6 us (8%)
  starting transfers between devices  37.9 us (8%)
  between operations  14.9 us (3%)
    unnamed x3, other arithmetic  149 us
    psum x1, waiting for transfers between devices, channel_layout(): grad_time = lax.psum(jnp.transpose(joined[spread:], (1, 0)), 'dp')  80 us
    unnamed x49, local copies, waits for them, and re-layouts  51.3 us
    all_to_all x1, local copies, waits for them, and re-layouts, channel_layout(): lax.all_to_all(grad_time[None], 'seq', split_axis=1, concat_axis=2, tiled...  15 us
    psum x1, local copies, waits for them, and re-layouts, channel_layout(): grad_time = lax.psum(jnp.transpose(joined[spread:], (1, 0)), 'dp')  14.8 us
    all_to_all x1, starting transfers between devices, channel_layout(): lax.all_to_all(weighted, 'seq', split_axis=2, concat_axis=1, tiled=True)  14.5 us
    transpose x1, local copies, waits for them, and re-layouts, channel_layout(): jnp.transpose(joined[:spread].reshape(batch_local, narrow, length), (0, 2...  12 us
    all_to_all x1, waiting for transfers between devices, channel_layout(): lax.all_to_all(weighted, 'seq', split_axis=2, concat_axis=1, tiled=True)  11.8 us
  transfers between devices with their start and end apart: 6, of which 4 were waited for; matrix products, arithmetic and copies ran while one was open for 26% of the time, Pallas kernels for 0%

commit v1 on v0

v1 whole, which is shorter than its diff:
```python
import functools
import math

import jax
import jax.numpy as jnp
import ml_dtypes
import numpy as np
from jax import lax
from jax.experimental import pallas as pl
from jax.experimental.pallas import tpu as pltpu
from jax.sharding import PartitionSpec as P

MESH = pl.DeviceIdType.MESH
F32 = jnp.float32
BF16 = jnp.bfloat16
LENGTH = 16384
PADDED = 2 * LENGTH


def halves(matrix):
    high = matrix.astype(ml_dtypes.bfloat16)
    low = (matrix - high.astype(np.float64)).astype(ml_dtypes.bfloat16)
    return np.stack([high, low])


def tables():
    freq = np.arange(128) + 0.5
    yx, zh, j = np.meshgrid(np.arange(16), np.arange(2), np.arange(4), indexing="ij")
    natural = (8 * yx + 4 * zh + j).reshape(-1)

    def outer(n1):
        phase = 2.0 * math.pi / 256.0 * ((n1[None, :] * freq[:, None]) % 256.0)
        return np.concatenate([np.cos(phase), -np.sin(phase)], axis=0)

    zh2, yx2, which, j2 = np.meshgrid(
        np.arange(2), np.arange(16), np.arange(2), np.arange(4), indexing="ij"
    )
    n1 = (8 * yx2 + 4 * zh2 + j2).reshape(-1)
    which = which.reshape(-1)
    base = outer(n1)
    pair = np.concatenate([base * (which == 0), base * (which == 1)], axis=0)
    yx3, side, j3 = np.meshgrid(np.arange(16), np.arange(2), np.arange(4), indexing="ij")
    taps = [
        halves(outer((8 * yx3 + 4 * (side ^ own) + j3).reshape(-1))) for own in range(2)
    ]
    turn = 2.0 * math.pi / PADDED * (np.arange(128)[None, :] * freq[:, None])
    twiddle = np.stack([np.cos(turn), np.sin(turn)]).astype(np.float32)
    inner = 2.0 * math.pi / 128.0 * (np.arange(128)[:, None] * np.arange(128)[None, :] % 128)
    cosine, sine = np.cos(inner), np.sin(inner)
    ahead = np.block([[cosine, -sine], [sine, cosine]])
    back = np.block([[cosine, sine], [-sine, cosine]])
    finish = outer(natural).T * (2.0 / PADDED)
    return halves(pair), np.stack(taps), halves(ahead), halves(back), halves(finish), twiddle


def split(x):
    high = x.astype(BF16)
    return high, (x - high.astype(F32)).astype(BF16)


def dot(a, b):
    return jnp.dot(a, b, preferred_element_type=F32)


def left(matrix, x):
    high, low = split(x)
    return dot(matrix[0], high) + (dot(matrix[0], low) + dot(matrix[1], high))


def right(x, matrix):
    high, low = split(x)
    return dot(high, matrix[0]) + (dot(low, matrix[0]) + dot(high, matrix[1]))


def kernel(
    first, value, gate, cot, taps, skip, m_pair, m_taps, m_ahead, m_back, m_finish, twiddle,
    out, grad_out,
    tiles, taps_t, taps_out, taps_in, taps_own, taps_all, near, slots, conv, conv_in, conv_pack,
    conv_all, part, part_in, whole, grad_in, grad_pack, grad_all,
    s_taps, r_taps, s_txy, r_txy, s_xy, r_xy, s_z, r_z, s_own, s_bxy, r_bxy, s_bz, r_bz,
    s_sib, r_sib, s_gxy, r_gxy, s_gz, r_gz,
):
    dp, seq = lax.axis_index("dp"), lax.axis_index("seq")
    yx, zh, zl, core = seq // 2, seq % 2, dp // 2, dp % 2
    z = zh * 4 + zl
    y, x = yx // 4, yx % 4
    group = zl // 2
    lands = zh * 4 + (zl % 2) * 2 + core

    def device(yx_, z_, core_):
        return {"dp": (z_ % 4) * 2 + core_, "seq": yx_ * 2 + z_ // 4}

    def beside(i):
        return ((y + i // 4) % 4) * 4 + (x + i % 4) % 4

    def rows(start, count):
        return pl.ds(pl.multiple_of(start, 8), count)

    def remote(src, dst, send, recv, where):
        return pltpu.make_async_remote_copy(
            src_ref=src, dst_ref=dst, send_sem=send, recv_sem=recv, device_id=where, device_id_type=MESH
        )

    def arrived(ref, sem):
        pltpu.make_async_copy(ref, ref, sem).wait()

    entry = pltpu.get_barrier_semaphore()

    def greet_column(i, _):
        other = (z * 2 + core + i) % 16
        pl.semaphore_signal(entry, inc=1, device_id=device(yx, other // 2, other % 2), device_id_type=MESH)
        return 0

    def greet_plane(i, _):
        pl.semaphore_signal(entry, inc=1, device_id=device(beside(i), z, core), device_id_type=MESH)
        return 0

    lax.fori_loop(1, 16, greet_column, 0)
    lax.fori_loop(1, 16, greet_plane, 0)

    for j in range(4):
        block = pl.ds(128 * j, 128)
        g = first[block, :].astype(F32) * value[block, :].astype(F32)
        tiles[pl.ds(j, 128, stride=8), :] = g.T
        w = cot[block, :].astype(F32) * gate[block, :].astype(F32)
        tiles[pl.ds(4 + j, 128, stride=8), :] = w.T
        taps_t[block, :] = taps[block, :].T
    across = (z + 4) % 8
    for j in range(4):
        taps_own[pl.ds(j, 16, stride=8), :] = taps_t[rows(128 * j + 16 * z, 16), :]
        taps_out[pl.ds(j, 16, stride=4), :] = taps_t[rows(128 * j + 16 * across, 16), :]

    pl.semaphore_wait(entry, 30)

    def to_plane(dz):
        zt = (z + dz) % 8
        pltpu.make_async_copy(tiles.at[rows((zt * 16 + yx) * 8, 8)], near.at[yx, zt], r_xy.at[zt]).start()

        def step(i, _):
            there = beside(i)
            remote(
                tiles.at[rows((zt * 16 + there) * 8, 8)], near.at[yx, zt], s_xy, r_xy.at[zt], device(there, z, core)
            ).start()
            return 0

        lax.fori_loop(1, 16, step, 0)

    def to_column(dz):
        zt = (z + dz) % 8
        arrived(near.at[:, zt], r_xy.at[zt])
        if dz:
            remote(near.at[:, zt], slots.at[lands], s_z, r_z.at[lands], device(yx, zt, group)).start()
            return

        @pl.when(group == core)
        def _():
            pltpu.make_async_copy(near.at[:, zt], slots.at[lands], r_z.at[lands]).start()

        @pl.when(group != core)
        def _():
            remote(near.at[:, zt], slots.at[lands], s_own, r_z.at[lands], device(yx, z, 1 - core)).start()

    remote(taps_out, taps_in, s_taps, r_taps, device(yx, across, core)).start()
    order = (4, 3, 5, 2, 6, 1, 7, 0)
    lag = 2
    for i in range(8 + lag):
        if i < 8:
            to_plane(order[i])
        if i >= lag:
            to_column(order[i - lag])

    arrived(taps_in, r_taps)
    for j in range(4):
        taps_own[pl.ds(4 + j, 16, stride=8), :] = taps_in[pl.ds(j, 16, stride=4), :]

    def spread(src, dst, base, send, recv):
        pltpu.make_async_copy(src.at[rows(base + yx * 8, 8)], dst.at[rows(base + yx * 8, 8)], recv).start()

        def step(i, _):
            there = beside(i)
            remote(
                src.at[rows(base + there * 8, 8)], dst.at[rows(base + yx * 8, 8)], send, recv, device(there, z, core)
            ).start()
            return 0

        lax.fori_loop(1, 16, step, 0)

    spread(taps_own, taps_all, 0, s_txy, r_txy)
    cosine, sine = twiddle[0], twiddle[1]

    def turned(re, im):
        return jnp.concatenate([re * cosine + im * sine, im * cosine - re * sine], axis=1)

    def inverse(re, im):
        d = right(jnp.concatenate([re, im], axis=1), m_back)
        dr, di = d[:, :128], d[:, 128:]
        e = jnp.concatenate([dr * cosine - di * sine, di * cosine + dr * sine], axis=0)
        return left(m_finish, e)

    arrived(taps_all, r_txy)
    a = left(m_taps.at[zh], taps_all[...])
    h = right(turned(a[:128], a[128:]), m_ahead)
    hr, hi = h[:, :128], h[:, 128:]

    def pack(src, base, dst, to):
        for side in range(2):
            for j in range(4):
                dst[pl.ds(to + 64 * side + j, 16, stride=4), :] = src[pl.ds(base + 4 * side + j, 16, stride=8), :]

    def home(bq):
        arrived(conv_in.at[pl.ds(128 * bq, 128)], r_bxy.at[bq])
        pack(conv_in, 128 * bq, conv_pack, 128 * bq)
        for side in range(2):
            z_to, core_to = 4 * side + 2 * core + bq // 2, bq % 2
            mine = jnp.logical_and(z_to == z, core_to == core)
            src = conv_pack.at[pl.ds(128 * bq + 64 * side, 64)]
            dst = conv_all.at[rows(64 * z, 64)]

            @pl.when(mine)
            def _():
                pltpu.make_async_copy(src, dst, r_bz).start()

            @pl.when(jnp.logical_not(mine))
            def _():
                remote(src, dst, s_bz, r_bz, device(yx, z_to, core_to)).start()

    total_re = total_im = None
    for bq in range(4):
        arrived(slots.at[bq], r_z.at[bq])
        arrived(slots.at[4 + bq], r_z.at[4 + bq])
        rows_in = jnp.concatenate([slots[bq].reshape(128, 128), slots[4 + bq].reshape(128, 128)], axis=0)
        a = left(m_pair, rows_in)
        b = jnp.concatenate([turned(a[:128], a[128:256]), turned(a[256:384], a[384:])], axis=0)
        s = right(b, m_ahead)
        gr, gi, wr, wi = s[:128, :128], s[:128, 128:], s[128:, :128], s[128:, 128:]
        qr, qi = wr * gr + wi * gi, wi * gr - wr * gi
        total_re = qr if bq == 0 else total_re + qr
        total_im = qi if bq == 0 else total_im + qi
        conv[pl.ds(128 * bq, 128), :] = inverse(gr * hr - gi * hi, gr * hi + gi * hr)
        spread(conv, conv_in, 128 * bq, s_bxy, r_bxy.at[bq])
        if bq:
            home(bq - 1)

    part[...] = inverse(total_re, total_im)
    sibling = remote(part, part_in, s_sib, r_sib, device(yx, z, 1 - core))
    sibling.start()
    home(3)
    arrived(part_in, r_sib)
    whole[...] = (part[...] + part_in[...]) * (1.0 / math.sqrt(8 * LENGTH))
    spread(whole, grad_in, 0, s_gxy, r_gxy)
    arrived(grad_in, r_gxy)
    pack(grad_in, 0, grad_pack, 0)
    pltpu.make_async_copy(grad_pack.at[rows(64 * zh, 64)], grad_all.at[rows(64 * z, 64)], r_gz).start()
    for dz in range(1, 8):
        zt = (z + dz) % 8
        remote(
            grad_pack.at[rows(64 * (zt // 4), 64)], grad_all.at[rows(64 * z, 64)], s_gz, r_gz, device(yx, zt, core)
        ).start()

    arrived(conv_all, r_bz)
    for j in range(4):
        block = pl.ds(128 * j, 128)
        g = first[block, :].astype(F32) * value[block, :].astype(F32)
        c = conv_all[pl.ds(j, 128, stride=4), :].T
        out[block, :] = (gate[block, :].astype(F32) * (c + skip[...] * g)).astype(BF16)
    arrived(grad_all, r_gz)
    for j in range(4):
        grad_out[pl.ds(128 * j, 128), :] = grad_all[pl.ds(j, 128, stride=4), :].T

    arrived(taps_out, s_taps)
    arrived(taps_own.at[pl.ds(0, 120)], s_txy)
    arrived(tiles.at[pl.ds(0, 960)], s_xy)
    arrived(slots.at[pl.ds(0, 7)], s_z)
    arrived(conv.at[pl.ds(0, 480)], s_bxy)
    arrived(conv_pack.at[pl.ds(0, 448)], s_bz)

    @pl.when(group != core)
    def _():
        arrived(slots.at[0], s_own)
        arrived(conv_pack.at[pl.ds(0, 64)], s_bz)

    arrived(part, s_sib)
    arrived(whole.at[pl.ds(0, 120)], s_gxy)
    arrived(grad_all.at[pl.ds(0, 448)], s_gz)


def shards(first_input, value_input, gate_input, cotangent, filter_taps, skip_weight):
    constants = tables()
    vmem = pl.BlockSpec(memory_space=pltpu.VMEM)
    dma = pltpu.SemaphoreType.DMA
    square = pltpu.VMEM((128, 128), F32)
    tall = pltpu.VMEM((512, 128), F32)
    short = pltpu.VMEM((64, 128), F32)
    out, grad = pl.pallas_call(
        kernel,
        out_shape=(
            jax.ShapeDtypeStruct((512, 128), BF16),
            jax.ShapeDtypeStruct((512, 128), F32),
        ),
        in_specs=[vmem] * 12,
        out_specs=(vmem, vmem),
        scratch_shapes=[
            pltpu.VMEM((1024, 128), F32),
            tall,
            short, short, square, square,
            pltpu.VMEM((16, 8, 8, 128), F32),
            pltpu.VMEM((8, 16, 8, 128), F32),
            tall, tall, tall, tall,
            square, square, square, square, square,
            tall,
            dma, dma, dma, dma, dma, dma((8,)), dma, dma((8,)), dma, dma, dma((4,)), dma, dma,
            dma, dma, dma, dma, dma, dma,
        ],
        compiler_params=pltpu.CompilerParams(
            collective_id=1, has_side_effects=True, vmem_limit_bytes=48 * 2**20
        ),
        name="hyena",
    )(
        first_input[0], value_input[0], gate_input[0], cotangent[0], filter_taps, skip_weight[None],
        *[jnp.asarray(c) for c in constants],
    )
    return out[None], grad


def solution(mesh):
    long, filt = P("dp", "seq", None), P("seq", None)
    return jax.shard_map(
        shards,
        mesh=mesh,
        in_specs=(long, long, long, long, filt, P()),
        out_specs=(long, filt),
        check_vma=False,
    )
```

time: 491 us -> 69.4 us (0.14)
  other arithmetic: 160 us -> 0 us
  waiting for transfers between devices: 112 us -> 0 us
  local copies, waits for them, and re-layouts: 120 us -> 12.3 us
  Pallas kernels: 0 us -> 56.1 us
  matrix products: 41.6 us -> 0 us
  starting transfers between devices: 37.9 us -> 0 us
  between operations: 14.9 us -> 0.66 us
    unnamed x3 -> x0, other arithmetic: 149 us -> none
    psum x1 -> x0, waiting for transfers between devices: 80 us -> none  [channel_layout(): grad_time = lax.psum(jnp.transpose(joined[spread:], (1, 0)), 'dp')]
    pallas_call x0 -> x1, Pallas kernels: none -> 56.1 us  [shards(): pl.pallas_call(kernel, out_shape=(jax.ShapeDtypeStruct((512, 128), BF16),...]
    dot_general x16 -> x0, matrix products: 41.6 us -> none  [the longest x2 7.38 us: local_transform(): mix('ckq,jq->ckj', section_imag, second_sin)]
    unnamed x49 -> x26, local copies, waits for them, and re-layouts: 51.3 us -> 12.3 us
    all_to_all x5 -> x0, starting transfers between devices: 37.9 us -> none  [the longest x1 14.5 us: channel_layout(): lax.all_to_all(weighted, 'seq', split_axis=2, concat_axis=1, tiled=True)]
    all_to_all x5 -> x0, waiting for transfers between devices: 30.9 us -> none  [the longest x1 11.8 us: channel_layout(): lax.all_to_all(weighted, 'seq', split_axis=2, concat_axis=1, tiled=True)]
    all_to_all x9 -> x0, local copies, waits for them, and re-layouts: 21.3 us -> none  [the longest x1 15 us: channel_layout(): lax.all_to_all(grad_time[None], 'seq', split_axis=1, concat_axis=2, tiled...]
  transfers between devices with their start and end apart: 6 -> 0, of which waited for: 4 -> 0; matrix products, arithmetic and copies ran while one was open for 26% -> 0% of each run, Pallas kernels for 0% -> 0%
where the time goes in v1:
time: 69.4 us; the launch traced here: 69.1 us
  Pallas kernels  56.1 us (81%)
  local copies, waits for them, and re-layouts  12.3 us (18%)
    pallas_call x1, Pallas kernels, shards(): pl.pallas_call(kernel, out_shape=(jax.ShapeDtypeStruct((512, 128), BF16),...  56.1 us
    unnamed x26, local copies, waits for them, and re-layouts  12.3 us

profile of v1, /device:TPU:1, one launch (start us, length us, event | category | flops | bytes accessed | tf_op | source)
XLA Modules:
  0.0 69.1 jit_solution(3731347869846441291)
XLA Ops:
  0.6 0.0 copy-start.11
  0.6 0.6 copy-done.11
  1.3 0.0 copy-start
  1.3 1.0 %copy-done = bf16[2,512,256]{2,1,0:T(8,128)(2,1)S(1)} copy-done((bf16[2,512,256]{2,1,0:T(8,128)(2,1)S(1)}, bf16[2,512,256]{2,1,0:T(8,128)(2,1)}, u32[]{:S(2)}) %copy-start) | copy-done | bytes 524312
  2.3 0.0 copy-start.1
  2.3 0.9 %copy-done.1 = f32[512,128]{1,0:T(8,128)S(1)} copy-done((f32[512,128]{1,0:T(8,128)S(1)}, f32[512,128]{1,0:T(8,128)}, u32[]{:S(2)}) %copy-start.1) | copy-done | bytes 262168
  3.3 0.0 copy-start.2
  3.3 0.9 %copy-done.2 = bf16[2,256,256]{2,1,0:T(8,128)(2,1)S(1)} copy-done((bf16[2,256,256]{2,1,0:T(8,128)(2,1)S(1)}, bf16[2,256,256]{2,1,0:T(8,128)(2,1)}, u32[]{:S(2)}) %copy-start.2) | copy-done | bytes 262168
  4.2 0.0 copy-start.3
  4.2 0.9 %copy-done.3 = bf16[2,256,256]{2,1,0:T(8,128)(2,1)S(1)} copy-done((bf16[2,256,256]{2,1,0:T(8,128)(2,1)S(1)}, bf16[2,256,256]{2,1,0:T(8,128)(2,1)}, u32[]{:S(2)}) %copy-start.3) | copy-done | bytes 262168
  5.2 0.0 copy-start.4
  5.2 0.9 %copy-done.4 = bf16[2,2,256,128]{3,2,1,0:T(8,128)(2,1)S(1)} copy-done((bf16[2,2,256,128]{3,2,1,0:T(8,128)(2,1)S(1)}, bf16[2,2,256,128]{3,2,1,0:T(8,128)(2,1)}, u32[]{:S(2)}) %copy-start.4) | copy-done | bytes 262168
  6.1 0.0 copy-start.5
  6.1 0.9 %copy-done.5 = bf16[1,512,128]{2,1,0:T(8,128)(2,1)S(1)} copy-done((bf16[1,512,128]{2,1,0:T(8,128)(2,1)S(1)}, bf16[1,512,128]{2,1,0:T(8,128)(2,1)}, u32[]{:S(2)}) %copy-start.5) | copy-done | bytes 131096
  7.0 0.0 copy-start.6
  7.0 0.9 %copy-done.6 = bf16[1,512,128]{2,1,0:T(8,128)(2,1)S(1)} copy-done((bf16[1,512,128]{2,1,0:T(8,128)(2,1)S(1)}, bf16[1,512,128]{2,1,0:T(8,128)(2,1)}, u32[]{:S(2)}) %copy-start.6) | copy-done | bytes 131096
  7.9 0.0 copy-start.7
  7.9 0.9 %copy-done.7 = bf16[1,512,128]{2,1,0:T(8,128)(2,1)S(1)} copy-done((bf16[1,512,128]{2,1,0:T(8,128)(2,1)S(1)}, bf16[1,512,128]{2,1,0:T(8,128)(2,1)}, u32[]{:S(2)}) %copy-start.7) | copy-done | bytes 131096
  8.8 0.9 %copy-done.8 = bf16[1,512,128]{2,1,0:T(8,128)(2,1)S(1)} copy-done((bf16[1,512,128]{2,1,0:T(8,128)(2,1)S(1)}, bf16[1,512,128]{2,1,0:T(8,128)(2,1)}, u32[]{:S(2)}) %copy-start.8) | copy-done | bytes 131096
  9.8 0.9 %copy-done.9 = f32[2,128,128]{2,1,0:T(8,128)S(1)} copy-done((f32[2,128,128]{2,1,0:T(8,128)S(1)}, f32[2,128,128]{2,1,0:T(8,128)}, u32[]{:S(2)}) %copy-start.9) | copy-done | bytes 131096
  10.7 0.9 %copy-done.10 = bf16[2,128,256]{2,1,0:T(8,128)(2,1)S(1)} copy-done((bf16[2,128,256]{2,1,0:T(8,128)(2,1)S(1)}, bf16[2,128,256]{2,1,0:T(8,128)(2,1)}, u32[]{:S(2)}) %copy-start.10) | copy-done | bytes 131096
  11.6 56.1 %hyena.1 = (bf16[512,128]{1,0:T(8,128)(2,1)S(1)}, f32[512,128]{1,0:T(8,128)S(1)}) custom-call(bf16[512,128]{1,0:T(8,128)(2,1)S(1)} %bitcast.6, bf16[512,128]{1,0:T(8,128)(2,1)S(1)} %bitcast.7, bf16[512,128]{1,0:T(8,128)(2,1)S(1)} %bitcast.8, bf16[512,128]{1,0:T(8,128)(2,1)S(1)} %bitcast.9, f32[512,128]{1,0:T(8,128)S(1)} %copy-done.1, f32[1,128]{1,0:T(1,128)S(1)} %bitcast.11, ...), custom_call_target="tpu_custom_call" | custom-call | tf_op jit(solution)/shard_map/hyena/pallas_call | solution.py:294
  67.7 0.7 copy.16
  68.4 0.7 %copy.17 = f32[512,128]{1,0:T(8,128)} copy(f32[512,128]{1,0:T(8,128)S(1)} %get-tuple-element.9) | data formatting | bytes 524288
  (3 shorter events, 0.0 us)
Async XLA Ops:
  0.6 0.7 copy-start.11
  1.3 1.0 %copy-start = (bf16[2,512,256]{2,1,0:T(8,128)(2,1)S(1)}, bf16[2,512,256]{2,1,0:T(8,128)(2,1)}, u32[]{:S(2)}) copy-start(bf16[2,512,256]{2,1,0:T(8,128)(2,1)} %constant.12.clone.m_pair) | copy-start | bytes 1572868
  2.3 0.9 %copy-start.1 = (f32[512,128]{1,0:T(8,128)S(1)}, f32[512,128]{1,0:T(8,128)}, u32[]{:S(2)}) copy-start(f32[512,128]{1,0:T(8,128)} %taps.1) | copy-start | bytes 786436
  3.3 0.9 %copy-start.2 = (bf16[2,256,256]{2,1,0:T(8,128)(2,1)S(1)}, bf16[2,256,256]{2,1,0:T(8,128)(2,1)}, u32[]{:S(2)}) copy-start(bf16[2,256,256]{2,1,0:T(8,128)(2,1)} %constant.15.clone.m_back) | copy-start | bytes 786436
  4.2 0.9 %copy-start.3 = (bf16[2,256,256]{2,1,0:T(8,128)(2,1)S(1)}, bf16[2,256,256]{2,1,0:T(8,128)(2,1)}, u32[]{:S(2)}) copy-start(bf16[2,256,256]{2,1,0:T(8,128)(2,1)} %constant.14.clone.m_ahead) | copy-start | bytes 786436
  5.2 0.9 %copy-start.4 = (bf16[2,2,256,128]{3,2,1,0:T(8,128)(2,1)S(1)}, bf16[2,2,256,128]{3,2,1,0:T(8,128)(2,1)}, u32[]{:S(2)}) copy-start(bf16[2,2,256,128]{3,2,1,0:T(8,128)(2,1)} %constant.13.clone.m_taps) | copy-start | bytes 786436
  6.1 0.9 %copy-start.5 = (bf16[1,512,128]{2,1,0:T(8,128)(2,1)S(1)}, bf16[1,512,128]{2,1,0:T(8,128)(2,1)}, u32[]{:S(2)}) copy-start(bf16[1,512,128]{2,1,0:T(8,128)(2,1)} %param.12) | copy-start | bytes 393220
  7.0 0.9 %copy-start.6 = (bf16[1,512,128]{2,1,0:T(8,128)(2,1)S(1)}, bf16[1,512,128]{2,1,0:T(8,128)(2,1)}, u32[]{:S(2)}) copy-start(bf16[1,512,128]{2,1,0:T(8,128)(2,1)} %param.13) | copy-start | bytes 393220
  7.9 0.9 %copy-start.7 = (bf16[1,512,128]{2,1,0:T(8,128)(2,1)S(1)}, bf16[1,512,128]{2,1,0:T(8,128)(2,1)}, u32[]{:S(2)}) copy-start(bf16[1,512,128]{2,1,0:T(8,128)(2,1)} %param.14) | copy-start | bytes 393220
  8.8 0.9 %copy-start.8 = (bf16[1,512,128]{2,1,0:T(8,128)(2,1)S(1)}, bf16[1,512,128]{2,1,0:T(8,128)(2,1)}, u32[]{:S(2)}) copy-start(bf16[1,512,128]{2,1,0:T(8,128)(2,1)} %param.15) | copy-start | bytes 393220
  9.8 0.9 %copy-start.9 = (f32[2,128,128]{2,1,0:T(8,128)S(1)}, f32[2,128,128]{2,1,0:T(8,128)}, u32[]{:S(2)}) copy-start(f32[2,128,128]{2,1,0:T(8,128)} %constant.17.clone.twiddle) | copy-start | bytes 393220
  10.7 0.9 %copy-start.10 = (bf16[2,128,256]{2,1,0:T(8,128)(2,1)S(1)}, bf16[2,128,256]{2,1,0:T(8,128)(2,1)}, u32[]{:S(2)}) copy-start(bf16[2,128,256]{2,1,0:T(8,128)(2,1)} %constant.16.clone.m_finish) | copy-start | bytes 393220

commit v2 on v1

v2 whole, which is shorter than its diff:
```python
import functools
import math

import jax
import jax.numpy as jnp
import ml_dtypes
import numpy as np
from jax import lax
from jax.experimental import pallas as pl
from jax.experimental.pallas import tpu as pltpu
from jax.sharding import PartitionSpec as P

MESH = pl.DeviceIdType.MESH
F32 = jnp.float32
BF16 = jnp.bfloat16
LENGTH = 16384
PADDED = 2 * LENGTH


def halves(matrix):
    high = matrix.astype(ml_dtypes.bfloat16)
    low = (matrix - high.astype(np.float64)).astype(ml_dtypes.bfloat16)
    return np.stack([high, low])


def tables():
    freq = np.arange(128) + 0.5

    def outer(*axes):
        yx, zh, j = (a.reshape(-1) for a in np.broadcast_arrays(*axes))
        n1 = 8 * yx + 4 * zh + j
        phase = 2.0 * math.pi / 256.0 * ((n1[None, :] * freq[:, None]) % 256.0)
        return np.concatenate([np.cos(phase), -np.sin(phase)], axis=0)

    a16, a2, a4 = np.arange(16), np.arange(2), np.arange(4)
    signal = outer(a16[None, :, None], a2[:, None, None], a4)
    taps = [halves(outer(a16[:, None, None], a2[:, None] ^ own, a4)) for own in range(2)]
    turn = 2.0 * math.pi / PADDED * (np.arange(128)[None, :] * freq[:, None])
    twiddle = np.stack([np.cos(turn), np.sin(turn)]).astype(np.float32)
    inner = 2.0 * math.pi / 128.0 * (np.arange(128)[:, None] * np.arange(128)[None, :] % 128)
    cosine, sine = np.cos(inner), np.sin(inner)
    ahead = np.block([[cosine, -sine], [sine, cosine]])
    back = np.block([[cosine, sine], [-sine, cosine]])
    finish = outer(a16[:, None, None], a2[:, None], a4).T * (2.0 / PADDED)
    return halves(signal), np.stack(taps), halves(ahead), halves(back), halves(finish), twiddle


def split(x):
    high = x.astype(BF16)
    return high, (x - high.astype(F32)).astype(BF16)


def dot(a, b):
    return jnp.dot(a, b, preferred_element_type=F32)


def left(matrix, x):
    high, low = split(x)
    return dot(matrix[0], high) + (dot(matrix[0], low) + dot(matrix[1], high))


def right(x, matrix):
    high, low = split(x)
    return dot(high, matrix[0]) + (dot(low, matrix[0]) + dot(high, matrix[1]))


def kernel(
    first_h, value_h, gate_h, cot_h, taps_h, skip, signal_h, taps_mh, ahead_h, back_h, finish_h, twiddle_h,
    out, grad_out,
    first, value, gate, cot, taps, m_signal, m_taps, m_ahead, m_back, m_finish, twiddle,
    tiles_g, tiles_w, near_g, near_w, column_g, column_w, slots_g, slots_w,
    taps_t, taps_out, taps_in, taps_own, taps_all, spectra,
    conv, conv_in, conv_pack, conv_all, part, part_in, whole, grad_in, grad_pack, grad_all,
    loads, s_taps, r_taps, s_txy, r_txy, s_xy, r_xy, s_z, r_z, s_bxy, r_bxy, s_bz, r_bz,
    s_sib, r_sib, s_gxy, r_gxy, s_gz, r_gz, s_last, r_last,
):
    dp, seq = lax.axis_index("dp"), lax.axis_index("seq")
    yx, zh, zl, core = seq // 2, seq % 2, dp // 2, dp % 2
    z = zh * 4 + zl
    y, x = yx // 4, yx % 4
    group = zl // 2
    stays = group == core
    lands = zh * 4 + (zl % 2) * 2 + core

    def device(yx_, z_, core_):
        return {"dp": (z_ % 4) * 2 + core_, "seq": yx_ * 2 + z_ // 4}

    def beside(i):
        return ((y + i // 4) % 4) * 4 + (x + i % 4) % 4

    def rows(start, count):
        return pl.ds(pl.multiple_of(start, 8), count)

    def remote(src, dst, send, recv, where):
        return pltpu.make_async_remote_copy(
            src_ref=src, dst_ref=dst, send_sem=send, recv_sem=recv, device_id=where, device_id_type=MESH
        )

    def arrived(ref, sem):
        pltpu.make_async_copy(ref, ref, sem).wait()

    def send_or_keep(mine, src, dst, send, recv, where):
        @pl.when(mine)
        def _():
            pltpu.make_async_copy(src, dst, recv).start()

        @pl.when(jnp.logical_not(mine))
        def _():
            remote(src, dst, send, recv, where).start()

    copies = [
        pltpu.make_async_copy(src, dst, loads.at[i])
        for i, (src, dst) in enumerate([
            (first_h.at[0], first), (value_h.at[0], value), (cot_h.at[0], cot), (gate_h.at[0], gate),
            (taps_h, taps), (signal_h, m_signal), (taps_mh, m_taps), (ahead_h, m_ahead),
            (back_h, m_back), (finish_h, m_finish), (twiddle_h, twiddle),
        ])
    ]
    for c in copies[:5]:
        c.start()

    entry = pltpu.get_barrier_semaphore()

    def greet_column(i, _):
        other = (z * 2 + core + i) % 16
        pl.semaphore_signal(entry, inc=1, device_id=device(yx, other // 2, other % 2), device_id_type=MESH)
        return 0

    def greet_plane(i, _):
        pl.semaphore_signal(entry, inc=1, device_id=device(beside(i), z, core), device_id_type=MESH)
        return 0

    lax.fori_loop(1, 16, greet_column, 0, unroll=True)
    lax.fori_loop(1, 16, greet_plane, 0, unroll=True)

    def product(a, b, dst):
        for j in range(4):
            block = pl.ds(128 * j, 128)
            p = (a[block, :].astype(F32) * b[block, :].astype(F32)).T
            for zt in range(8):
                dst[pl.ds(zt // 2 * 128 + zt % 2 * 4 + j, 16, stride=8), :] = p[16 * zt : 16 * zt + 16]

    copies[0].wait()
    copies[1].wait()
    product(first, value, tiles_g)
    pl.semaphore_wait(entry, 30)

    def to_plane(tiles, near, dq, which):
        base = (z // 2 + dq) % 4 * 128
        here = rows(dq * 128 + yx * 8, 8)
        recv = r_xy.at[4 * which + dq]
        pltpu.make_async_copy(tiles.at[rows(base + yx * 8, 8)], near.at[here], recv).start()

        def step(i, _):
            there = beside(i)
            remote(tiles.at[rows(base + there * 8, 8)], near.at[here], s_xy, recv, device(there, z, core)).start()
            return 0

        lax.fori_loop(1, 16, step, 0, unroll=True)

    def pack(src, base, dst, to):
        for side in range(2):
            for j in range(4):
                dst[pl.ds(to + 64 * side + j, 16, stride=4), :] = src[pl.ds(base + 4 * side + j, 16, stride=8), :]

    def to_column(near, column, slots, dq, which):
        arrived(near.at[pl.ds(dq * 128, 128)], r_xy.at[4 * which + dq])
        pack(near, dq * 128, column, dq * 128)
        for side in range(2):
            zt = (z // 2 + dq) % 4 * 2 + side
            src, dst, recv = column.at[pl.ds(dq * 128 + side * 64, 64)], slots.at[lands], r_z.at[8 * which + lands]
            if dq:
                remote(src, dst, s_z, recv, device(yx, zt, group)).start()
            else:
                send_or_keep(jnp.logical_and(zt == z, stays), src, dst, s_z, recv, device(yx, zt, group))

    order = (2, 1, 3, 0)
    for dq in order:
        to_plane(tiles_g, near_g, dq, 0)
    for c in copies[5:]:
        c.start()
    copies[4].wait()
    for j in range(4):
        block = pl.ds(128 * j, 128)
        taps_t[block, :] = taps[block, :].T
    across = (z + 4) % 8
    for j in range(4):
        taps_own[pl.ds(j, 16, stride=8), :] = taps_t[rows(128 * j + 16 * z, 16), :]
        taps_out[pl.ds(j, 16, stride=4), :] = taps_t[rows(128 * j + 16 * across, 16), :]
    remote(taps_out, taps_in, s_taps, r_taps, device(yx, across, core)).start()
    copies[2].wait()
    copies[3].wait()
    product(cot, gate, tiles_w)
    for dq in order:
        to_plane(tiles_w, near_w, dq, 1)
    for dq in order:
        to_column(near_g, column_g, slots_g, dq, 0)

    arrived(taps_in, r_taps)
    for j in range(4):
        taps_own[pl.ds(4 + j, 16, stride=8), :] = taps_in[pl.ds(j, 16, stride=4), :]

    def spread(src, dst, base, send, recv):
        here = rows(base + yx * 8, 8)
        pltpu.make_async_copy(src.at[here], dst.at[here], recv).start()

        def step(i, _):
            there = beside(i)
            remote(src.at[rows(base + there * 8, 8)], dst.at[here], send, recv, device(there, z, core)).start()
            return 0

        lax.fori_loop(1, 16, step, 0, unroll=True)

    spread(taps_own, taps_all, 0, s_txy, r_txy)
    for dq in order:
        to_column(near_w, column_w, slots_w, dq, 1)

    for c in copies[5:]:
        c.wait()
    cosine, sine = twiddle[0], twiddle[1]

    def forward(matrix, signal):
        a = left(matrix, signal)
        re, im = a[:128], a[128:]
        return right(jnp.concatenate([re * cosine + im * sine, im * cosine - re * sine], axis=1), m_ahead)

    def inverse(re, im):
        d = right(jnp.concatenate([re, im], axis=1), m_back)
        dr, di = d[:, :128], d[:, 128:]
        return left(m_finish, jnp.concatenate([dr * cosine - di * sine, di * cosine + dr * sine], axis=0))

    def spectrum(slots, bq, which):
        arrived(slots.at[bq], r_z.at[8 * which + bq])
        arrived(slots.at[4 + bq], r_z.at[8 * which + 4 + bq])
        return forward(m_signal, jnp.concatenate([slots[bq], slots[4 + bq]], axis=0))

    arrived(taps_all, r_txy)
    h = forward(m_taps.at[zh], taps_all[...])
    hr, hi = h[:, :128], h[:, 128:]

    def turn(i):
        return (i + z) % 4

    def home(i):
        bq = turn(i)
        arrived(conv_in.at[pl.ds(128 * i, 128)], r_bxy.at[i])
        pack(conv_in, 128 * i, conv_pack, 128 * i)
        for side in range(2):
            z_to, core_to = 4 * side + 2 * core + bq // 2, bq % 2
            send_or_keep(
                jnp.logical_and(z_to == z, core_to == core),
                conv_pack.at[pl.ds(128 * i + 64 * side, 64)], conv_all.at[rows(64 * z, 64)],
                s_bz, r_bz, device(yx, z_to, core_to),
            )

    for i in range(4):
        g = spectrum(slots_g, turn(i), 0)
        spectra[i] = g
        gr, gi = g[:, :128], g[:, 128:]
        conv[pl.ds(128 * i, 128), :] = inverse(gr * hr - gi * hi, gr * hi + gi * hr)
        spread(conv, conv_in, 128 * i, s_bxy, r_bxy.at[i])

    total_re = total_im = 0.0
    for i in range(4):
        w = spectrum(slots_w, turn(i), 1)
        wr, wi = w[:, :128], w[:, 128:]
        gr, gi = spectra[i, :, :128], spectra[i, :, 128:]
        total_re = total_re + (wr * gr + wi * gi)
        total_im = total_im + (wi * gr - wr * gi)

    part[...] = inverse(total_re, total_im)
    keeper = z % 2 == core
    sibling = device(yx, z, 1 - core)

    @pl.when(jnp.logical_not(keeper))
    def _():
        remote(part, part_in, s_sib, r_sib, sibling).start()

    home(0)
    home(1)

    @pl.when(keeper)
    def _():
        arrived(part_in, r_sib)
        whole[...] = (part[...] + part_in[...]) * (1.0 / math.sqrt(8 * LENGTH))
        spread(whole, grad_in, 0, s_gxy, r_gxy)

    home(2)

    @pl.when(keeper)
    def _():
        arrived(grad_in, r_gxy)
        pack(grad_in, 0, grad_pack, 0)
        pltpu.make_async_copy(grad_pack.at[rows(64 * zh, 64)], grad_all.at[z // 2, core], r_gz).start()

        def step(dz, _):
            zt = (z + dz) % 8
            remote(
                grad_pack.at[rows(64 * (zt // 4), 64)], grad_all.at[z // 2, core], s_gz, r_gz, device(yx, zt, core)
            ).start()
            return 0

        lax.fori_loop(1, 8, step, 0, unroll=True)

    home(3)
    arrived(grad_all.at[:, core], r_gz)
    last = remote(grad_all.at[:, core], grad_all.at[:, core], s_last, r_last, sibling)
    last.start()
    arrived(conv_all, r_bz)
    for j in range(4):
        block = pl.ds(128 * j, 128)
        g = first[block, :].astype(F32) * value[block, :].astype(F32)
        c = conv_all[pl.ds(j, 128, stride=4), :].T
        out[block, :] = (gate[block, :].astype(F32) * (c + skip[...] * g)).astype(BF16)

    arrived(grad_all.at[:, 1 - core], r_last)
    flat = grad_all[...].reshape(512, 128)
    taps_t[...] = flat
    for j in range(4):
        grad_out[pl.ds(128 * j, 128), :] = taps_t[pl.ds(j, 128, stride=4), :].T

    last.wait_send()
    arrived(taps_out, s_taps)
    arrived(taps_own.at[pl.ds(0, 120)], s_txy)
    arrived(tiles_g.at[pl.ds(0, 480)], s_xy)
    arrived(tiles_w.at[pl.ds(0, 480)], s_xy)
    arrived(column_g.at[pl.ds(0, 448)], s_z)
    arrived(column_w.at[pl.ds(0, 448)], s_z)
    arrived(conv.at[pl.ds(0, 480)], s_bxy)
    arrived(conv_pack.at[pl.ds(0, 448)], s_bz)

    @pl.when(jnp.logical_not(stays))
    def _():
        arrived(column_w.at[pl.ds(0, 128)], s_z)
        arrived(conv_pack.at[pl.ds(0, 64)], s_bz)

    @pl.when(jnp.logical_not(keeper))
    def _():
        arrived(part, s_sib)

    @pl.when(keeper)
    def _():
        arrived(whole.at[pl.ds(0, 120)], s_gxy)
        arrived(conv.at[pl.ds(0, 448)], s_gz)


def shards(first_input, value_input, gate_input, cotangent, filter_taps, skip_weight):
    constants = tables()
    vmem, hbm = pl.BlockSpec(memory_space=pltpu.VMEM), pl.BlockSpec(memory_space=pltpu.HBM)
    dma = pltpu.SemaphoreType.DMA
    square, tall, short = (pltpu.VMEM((n, 128), F32) for n in (128, 512, 64))
    operands = [
        first_input, value_input, gate_input, cotangent, filter_taps, skip_weight[None],
        *[jnp.asarray(c) for c in constants],
    ]
    long = pltpu.VMEM((512, 128), BF16)
    out, grad = pl.pallas_call(
        kernel,
        out_shape=(
            jax.ShapeDtypeStruct((512, 128), BF16),
            jax.ShapeDtypeStruct((512, 128), F32),
        ),
        in_specs=[hbm] * 5 + [vmem] + [hbm] * 6,
        out_specs=(vmem, vmem),
        scratch_shapes=[
            long, long, long, long, tall, *[pltpu.VMEM(c.shape, c.dtype) for c in constants],
            tall, tall, tall, tall, tall, tall,
            pltpu.VMEM((8, 64, 128), F32), pltpu.VMEM((8, 64, 128), F32),
            tall, short, short, square, square,
            pltpu.VMEM((4, 128, 256), F32),
            tall, tall, tall, tall,
            square, square, square, square, square,
            pltpu.VMEM((4, 2, 64, 128), F32),
            dma((11,)), dma, dma, dma, dma, dma, dma((8,)), dma, dma((16,)), dma, dma((4,)), dma, dma,
            dma, dma, dma, dma, dma, dma, dma, dma,
        ],
        compiler_params=pltpu.CompilerParams(
            collective_id=1, has_side_effects=True, vmem_limit_bytes=56 * 2**20
        ),
        name="hyena",
    )(*operands)
    return out[None], grad


def solution(mesh):
    long, filt = P("dp", "seq", None), P("seq", None)
    return jax.shard_map(
        shards,
        mesh=mesh,
        in_specs=(long, long, long, long, filt, P()),
        out_specs=(long, filt),
        check_vma=False,
    )
```

time: 69.4 us -> 49.2 us (0.71)
  Pallas kernels: 56.1 us -> 46.1 us
  local copies, waits for them, and re-layouts: 12.3 us -> 2.32 us
    pallas_call x1, Pallas kernels: 56.1 us -> 46.1 us  [shards(): pl.pallas_call(kernel, out_shape=(jax.ShapeDtypeStruct((512, 128), BF16),...]
    unnamed x26 -> x4, local copies, waits for them, and re-layouts: 12.3 us -> 2.32 us
where the time goes in v2:
time: 49.2 us; the launch traced here: 49.1 us
  Pallas kernels  46.1 us (94%)
  local copies, waits for them, and re-layouts  2.32 us (5%)
  between operations  0.65 us (1%)
    pallas_call x1, Pallas kernels, shards(): pl.pallas_call(kernel, out_shape=(jax.ShapeDtypeStruct((512, 128), BF16),...  46.1 us
    unnamed x4, local copies, waits for them, and re-layouts  2.32 us

profile of v2, /device:TPU:1, one launch (start us, length us, event | category | flops | bytes accessed | tf_op | source)
XLA Modules:
  0.0 49.1 jit_solution(558246417984482416)
XLA Ops:
  0.6 46.1 %hyena.1 = (bf16[512,128]{1,0:T(8,128)(2,1)}, f32[512,128]{1,0:T(8,128)}) custom-call(bf16[1,512,128]{2,1,0:T(8,128)(2,1)} %first_h.1, bf16[1,512,128]{2,1,0:T(8,128)(2,1)} %value_h.1, bf16[1,512,128]{2,1,0:T(8,128)(2,1)} %gate_h.1, bf16[1,512,128]{2,1,0:T(8,128)(2,1)} %cot_h.1, f32[512,128]{1,0:T(8,128)} %taps_h.1, f32[1,128]{1,0:T(1,128)} %bitcast.3, ...), custom_call_target="tpu_custom_call" | custom-call | tf_op jit(solution)/shard_map/hyena/pallas_call | solution.py:357
  46.8 0.0 copy-start
  46.8 1.6 %copy.16 = bf16[1,512,128]{2,1,0:T(8,128)(2,1)} copy(bf16[1,512,128]{2,1,0:T(8,128)(2,1)} %bitcast.2) | data formatting | bytes 262144
  48.4 0.0 copy-done
  48.4 0.7 %copy.17 = f32[512,128]{1,0:T(8,128)} copy(f32[512,128]{1,0:T(8,128)S(1)} %copy-done) | data formatting | bytes 524288
Async XLA Ops:
  46.8 1.6 %copy-start = (f32[512,128]{1,0:T(8,128)S(1)}, f32[512,128]{1,0:T(8,128)}, u32[]{:S(2)}) copy-start(f32[512,128]{1,0:T(8,128)} %get-tuple-element.9) | copy-start | bytes 786436

commit v3 on v2

--- a/solution.py
+++ b/solution.py
@@ -65,9 +65,9 @@
 
 
 def kernel(
-    first_h, value_h, gate_h, cot_h, taps_h, skip, signal_h, taps_mh, ahead_h, back_h, finish_h, twiddle_h,
-    out, grad_out,
-    first, value, gate, cot, taps, m_signal, m_taps, m_ahead, m_back, m_finish, twiddle,
+    first_h, value_h, gate_h, cot_h, taps_h, skip_h, signal_h, taps_mh, ahead_h, back_h, finish_h, twiddle_h,
+    out, grad_low, grad_high,
+    first, value, gate, cot, taps, skip, m_signal, m_taps, m_ahead, m_back, m_finish, twiddle,
     tiles_g, tiles_w, near_g, near_w, column_g, column_w, slots_g, slots_w,
     taps_t, taps_out, taps_in, taps_own, taps_all, spectra,
     conv, conv_in, conv_pack, conv_all, part, part_in, whole, grad_in, grad_pack, grad_all,
@@ -75,18 +75,23 @@
     s_sib, r_sib, s_gxy, r_gxy, s_gz, r_gz, s_last, r_last,
 ):
     dp, seq = lax.axis_index("dp"), lax.axis_index("seq")
-    yx, zh, zl, core = seq // 2, seq % 2, dp // 2, dp % 2
+    div, rem = lax.div, lax.rem
+    yx, zh, zl, core = div(seq, 2), rem(seq, 2), div(dp, 2), rem(dp, 2)
     z = zh * 4 + zl
-    y, x = yx // 4, yx % 4
-    group = zl // 2
+    y, x = div(yx, 4), rem(yx, 4)
+    group = div(zl, 2)
     stays = group == core
-    lands = zh * 4 + (zl % 2) * 2 + core
+    lands = zh * 4 + rem(zl, 2) * 2 + core
 
     def device(yx_, z_, core_):
-        return {"dp": (z_ % 4) * 2 + core_, "seq": yx_ * 2 + z_ // 4}
+        return {"dp": rem(z_, 4) * 2 + core_, "seq": yx_ * 2 + div(z_, 4)}
 
     def beside(i):
-        return ((y + i // 4) % 4) * 4 + (x + i % 4) % 4
+        return rem(y + i // 4, 4) * 4 + rem(x + i % 4, 4)
+
+    def plane(step):
+        for i in range(1, 16):
+            step(beside(i))
 
     def rows(start, count):
         return pl.ds(pl.multiple_of(start, 8), count)
@@ -112,7 +117,7 @@
         pltpu.make_async_copy(src, dst, loads.at[i])
         for i, (src, dst) in enumerate([
             (first_h.at[0], first), (value_h.at[0], value), (cot_h.at[0], cot), (gate_h.at[0], gate),
-            (taps_h, taps), (signal_h, m_signal), (taps_mh, m_taps), (ahead_h, m_ahead),
+            (taps_h, taps), (skip_h, skip), (signal_h, m_signal), (taps_mh, m_taps), (ahead_h, m_ahead),
             (back_h, m_back), (finish_h, m_finish), (twiddle_h, twiddle),
         ])
     ]
@@ -121,17 +126,13 @@
 
     entry = pltpu.get_barrier_semaphore()
 
-    def greet_column(i, _):
-        other = (z * 2 + core + i) % 16
-        pl.semaphore_signal(entry, inc=1, device_id=device(yx, other // 2, other % 2), device_id_type=MESH)
-        return 0
-
-    def greet_plane(i, _):
-        pl.semaphore_signal(entry, inc=1, device_id=device(beside(i), z, core), device_id_type=MESH)
-        return 0
-
-    lax.fori_loop(1, 16, greet_column, 0, unroll=True)
-    lax.fori_loop(1, 16, greet_plane, 0, unroll=True)
+    def greet(where):
+        pl.semaphore_signal(entry, inc=1, device_id=where, device_id_type=MESH)
+
+    for i in range(1, 16):
+        other = rem(z * 2 + core + i, 16)
+        greet(device(yx, div(other, 2), rem(other, 2)))
+    plane(lambda there: greet(device(there, z, core)))
 
     def product(a, b, dst):
         for j in range(4):
@@ -146,17 +147,15 @@
     pl.semaphore_wait(entry, 30)
 
     def to_plane(tiles, near, dq, which):
-        base = (z // 2 + dq) % 4 * 128
+        base = rem(div(z, 2) + dq, 4) * 128
         here = rows(dq * 128 + yx * 8, 8)
         recv = r_xy.at[4 * which + dq]
         pltpu.make_async_copy(tiles.at[rows(base + yx * 8, 8)], near.at[here], recv).start()
 
-        def step(i, _):
-            there = beside(i)
+        def step(there):
             remote(tiles.at[rows(base + there * 8, 8)], near.at[here], s_xy, recv, device(there, z, core)).start()
-            return 0
-
-        lax.fori_loop(1, 16, step, 0, unroll=True)
+
+        plane(step)
 
     def pack(src, base, dst, to):
         for side in range(2):
@@ -167,7 +166,7 @@
         arrived(near.at[pl.ds(dq * 128, 128)], r_xy.at[4 * which + dq])
         pack(near, dq * 128, column, dq * 128)
         for side in range(2):
-            zt = (z // 2 + dq) % 4 * 2 + side
+            zt = rem(div(z, 2) + dq, 4) * 2 + side
             src, dst, recv = column.at[pl.ds(dq * 128 + side * 64, 64)], slots.at[lands], r_z.at[8 * which + lands]
             if dq:
                 remote(src, dst, s_z, recv, device(yx, zt, group)).start()
@@ -183,7 +182,7 @@
     for j in range(4):
         block = pl.ds(128 * j, 128)
         taps_t[block, :] = taps[block, :].T
-    across = (z + 4) % 8
+    across = rem(z + 4, 8)
     for j in range(4):
         taps_own[pl.ds(j, 16, stride=8), :] = taps_t[rows(128 * j + 16 * z, 16), :]
         taps_out[pl.ds(j, 16, stride=4), :] = taps_t[rows(128 * j + 16 * across, 16), :]
@@ -204,12 +203,10 @@
         here = rows(base + yx * 8, 8)
         pltpu.make_async_copy(src.at[here], dst.at[here], recv).start()
 
-        def step(i, _):
-            there = beside(i)
+        def step(there):
             remote(src.at[rows(base + there * 8, 8)], dst.at[here], send, recv, device(there, z, core)).start()
-            return 0
-
-        lax.fori_loop(1, 16, step, 0, unroll=True)
+
+        plane(step)
 
     spread(taps_own, taps_all, 0, s_txy, r_txy)
     for dq in order:
@@ -239,14 +236,14 @@
     hr, hi = h[:, :128], h[:, 128:]
 
     def turn(i):
-        return (i + z) % 4
+        return rem(i + z, 4)
 
     def home(i):
         bq = turn(i)
         arrived(conv_in.at[pl.ds(128 * i, 128)], r_bxy.at[i])
         pack(conv_in, 128 * i, conv_pack, 128 * i)
         for side in range(2):
-            z_to, core_to = 4 * side + 2 * core + bq // 2, bq % 2
+            z_to, core_to = 4 * side + 2 * core + div(bq, 2), rem(bq, 2)
             send_or_keep(
                 jnp.logical_and(z_to == z, core_to == core),
                 conv_pack.at[pl.ds(128 * i + 64 * side, 64)], conv_all.at[rows(64 * z, 64)],
@@ -269,7 +266,7 @@
         total_im = total_im + (wi * gr - wr * gi)
 
     part[...] = inverse(total_re, total_im)
-    keeper = z % 2 == core
+    keeper = rem(z, 2) == core
     sibling = device(yx, z, 1 - core)
 
     @pl.when(jnp.logical_not(keeper))
@@ -291,16 +288,12 @@
     def _():
         arrived(grad_in, r_gxy)
         pack(grad_in, 0, grad_pack, 0)
-        pltpu.make_async_copy(grad_pack.at[rows(64 * zh, 64)], grad_all.at[z // 2, core], r_gz).start()
-
-        def step(dz, _):
-            zt = (z + dz) % 8
+        pltpu.make_async_copy(grad_pack.at[rows(64 * zh, 64)], grad_all.at[div(z, 2), core], r_gz).start()
+        for dz in (4, 3, 5, 2, 6, 1, 7):
+            zt = rem(z + dz, 8)
             remote(
-                grad_pack.at[rows(64 * (zt // 4), 64)], grad_all.at[z // 2, core], s_gz, r_gz, device(yx, zt, core)
+                grad_pack.at[rows(64 * div(zt, 4), 64)], grad_all.at[div(z, 2), core], s_gz, r_gz, device(yx, zt, core)
             ).start()
-            return 0
-
-        lax.fori_loop(1, 8, step, 0, unroll=True)
 
     home(3)
     arrived(grad_all.at[:, core], r_gz)
@@ -317,7 +310,7 @@
     flat = grad_all[...].reshape(512, 128)
     taps_t[...] = flat
     for j in range(4):
-        grad_out[pl.ds(128 * j, 128), :] = taps_t[pl.ds(j, 128, stride=4), :].T
+        (grad_low, grad_high)[j // 2][pl.ds(128 * (j % 2), 128), :] = taps_t[pl.ds(j, 128, stride=4), :].T
 
     last.wait_send()
     arrived(taps_out, s_taps)
@@ -354,16 +347,17 @@
         *[jnp.asarray(c) for c in constants],
     ]
     long = pltpu.VMEM((512, 128), BF16)
-    out, grad = pl.pallas_call(
+    out, low, high = pl.pallas_call(
         kernel,
         out_shape=(
             jax.ShapeDtypeStruct((512, 128), BF16),
-            jax.ShapeDtypeStruct((512, 128), F32),
+            jax.ShapeDtypeStruct((256, 128), F32),
+            jax.ShapeDtypeStruct((256, 128), F32),
         ),
-        in_specs=[hbm] * 5 + [vmem] + [hbm] * 6,
-        out_specs=(vmem, vmem),
+        in_specs=[hbm] * 12,
+        out_specs=(vmem, vmem, vmem),
         scratch_shapes=[
-            long, long, long, long, tall, *[pltpu.VMEM(c.shape, c.dtype) for c in constants],
+            long, long, long, long, tall, pltpu.VMEM((1, 128), F32), *[pltpu.VMEM(c.shape, c.dtype) for c in constants],
             tall, tall, tall, tall, tall, tall,
             pltpu.VMEM((8, 64, 128), F32), pltpu.VMEM((8, 64, 128), F32),
             tall, short, short, square, square,
@@ -371,15 +365,15 @@
             tall, tall, tall, tall,
             square, square, square, square, square,
             pltpu.VMEM((4, 2, 64, 128), F32),
-            dma((11,)), dma, dma, dma, dma, dma, dma((8,)), dma, dma((16,)), dma, dma((4,)), dma, dma,
+            dma((12,)), dma, dma, dma, dma, dma, dma((8,)), dma, dma((16,)), dma, dma((4,)), dma, dma,
             dma, dma, dma, dma, dma, dma, dma, dma,
         ],
         compiler_params=pltpu.CompilerParams(
-            collective_id=1, has_side_effects=True, vmem_limit_bytes=56 * 2**20
+            collective_id=1, has_side_effects=True, vmem_limit_bytes=56098816
         ),
         name="hyena",
     )(*operands)
-    return out[None], grad
+    return out[None], jnp.concatenate([low, high], axis=0)
 
 
 def solution(mesh):

time: 49.2 us -> 46.7 us (0.949)
  Pallas kernels: 46.1 us -> 43.9 us
  local copies, waits for them, and re-layouts: 2.32 us -> 1.3 us
  other arithmetic: 0 us -> 0.72 us
    pallas_call x1, Pallas kernels: 46.1 us -> 43.9 us  [shards(): pl.pallas_call(kernel, out_shape=(jax.ShapeDtypeStruct((512, 128), BF16),...]
    unnamed x4 -> x3, local copies, waits for them, and re-layouts: 2.32 us -> 1.3 us
    concatenate x0 -> x1, other arithmetic: none -> 0.72 us  [shards(): return (out[None], jnp.concatenate([low, high], axis=0))]
where the time goes in v3:
time: 46.7 us; the launch traced here: 46.6 us
  Pallas kernels  43.9 us (94%)
  local copies, waits for them, and re-layouts  1.3 us (3%)
  other arithmetic  0.72 us (2%)
  between operations  0.65 us (1%)
    pallas_call x1, Pallas kernels, shards(): pl.pallas_call(kernel, out_shape=(jax.ShapeDtypeStruct((512, 128), BF16),...  43.9 us
    unnamed x3, local copies, waits for them, and re-layouts  1.3 us

profile of v3, /device:TPU:1, one launch (start us, length us, event | category | flops | bytes accessed | tf_op | source)
XLA Modules:
  0.0 46.6 jit_solution(1835972093924604859)
XLA Ops:
  0.6 0.0 copy-start
  0.6 0.6 %copy-done = f32[128]{0:T(128)S(1)} copy-done((f32[128]{0:T(128)S(1)}, f32[128]{0:T(128)}, u32[]{:S(2)}) %copy-start) | copy-done | bytes 536
  1.3 43.9 %hyena.1 = (bf16[512,128]{1,0:T(8,128)(2,1)S(1)}, f32[256,128]{1,0:T(8,128)S(1)}, f32[256,128]{1,0:T(8,128)S(1)}) custom-call(bf16[1,512,128]{2,1,0:T(8,128)(2,1)} %first_h.1, bf16[1,512,128]{2,1,0:T(8,128)(2,1)} %value_h.1, bf16[1,512,128]{2,1,0:T(8,128)(2,1)} %gate_h.1, bf16[1,512,128]{2,1,0:T(8,128)(2,1)} %cot_h.1, f32[512,128]{1,0:T(8,128)} %taps_h.1, ...), custom_call_target="tpu_custom_call" | custom-call | tf_op jit(solution)/shard_map/hyena/pallas_call | solution.py:350
  45.2 0.7 %pad_maximum_fusion = f32[512,128]{1,0:T(8,128)} fusion(f32[256,128]{1,0:T(8,128)S(1)} %get-tuple-element.7, f32[256,128]{1,0:T(8,128)S(1)} %get-tuple-element.6), kind=kLoop, calls=%fused_computation | loop fusion | flops 65536 | bytes 524288 | tf_op jit(solution)/shard_map/concatenate | solution.py:376
  45.9 0.7 %copy.15 = bf16[1,512,128]{2,1,0:T(8,128)(2,1)} copy(bf16[1,512,128]{2,1,0:T(8,128)(2,1)S(1)} %bitcast.2) | data formatting | bytes 262144
Async XLA Ops:
  0.6 0.7 %copy-start = (f32[128]{0:T(128)S(1)}, f32[128]{0:T(128)}, u32[]{:S(2)}) copy-start(f32[128]{0:T(128)} %param.17) | copy-start | bytes 1540

commit v4 on v3

--- a/solution.py
+++ b/solution.py
@@ -65,9 +65,9 @@
 
 
 def kernel(
-    first_h, value_h, gate_h, cot_h, taps_h, skip_h, signal_h, taps_mh, ahead_h, back_h, finish_h, twiddle_h,
-    out, grad_low, grad_high,
-    first, value, gate, cot, taps, skip, m_signal, m_taps, m_ahead, m_back, m_finish, twiddle,
+    first_h, value_h, gate_h, cot_h, taps_h, signal_h, taps_mh, ahead_h, back_h, finish_h, twiddle_h,
+    filtered_low, filtered_high, direct_low, direct_high, grad_low, grad_high,
+    first, value, gate, cot, taps, m_signal, m_taps, m_ahead, m_back, m_finish, twiddle,
     tiles_g, tiles_w, near_g, near_w, column_g, column_w, slots_g, slots_w,
     taps_t, taps_out, taps_in, taps_own, taps_all, spectra,
     conv, conv_in, conv_pack, conv_all, part, part_in, whole, grad_in, grad_pack, grad_all,
@@ -117,7 +117,7 @@
         pltpu.make_async_copy(src, dst, loads.at[i])
         for i, (src, dst) in enumerate([
             (first_h.at[0], first), (value_h.at[0], value), (cot_h.at[0], cot), (gate_h.at[0], gate),
-            (taps_h, taps), (skip_h, skip), (signal_h, m_signal), (taps_mh, m_taps), (ahead_h, m_ahead),
+            (taps_h, taps), (signal_h, m_signal), (taps_mh, m_taps), (ahead_h, m_ahead),
             (back_h, m_back), (finish_h, m_finish), (twiddle_h, twiddle),
         ])
     ]
@@ -216,23 +216,37 @@
         c.wait()
     cosine, sine = twiddle[0], twiddle[1]
 
-    def forward(matrix, signal):
-        a = left(matrix, signal)
-        re, im = a[:128], a[128:]
-        return right(jnp.concatenate([re * cosine + im * sine, im * cosine - re * sine], axis=1), m_ahead)
-
-    def inverse(re, im):
-        d = right(jnp.concatenate([re, im], axis=1), m_back)
-        dr, di = d[:, :128], d[:, 128:]
-        return left(m_finish, jnp.concatenate([dr * cosine - di * sine, di * cosine + dr * sine], axis=0))
-
-    def spectrum(slots, bq, which):
+    def side_by_side(parts):
+        return jnp.concatenate(parts, axis=1) if len(parts) > 1 else parts[0]
+
+    def stacked(parts):
+        return jnp.concatenate(parts, axis=0) if len(parts) > 1 else parts[0]
+
+    def forward(matrix, signals):
+        a = left(matrix, side_by_side(signals))
+        turned = []
+        for i in range(len(signals)):
+            re, im = a[:128, 128 * i : 128 * i + 128], a[128:, 128 * i : 128 * i + 128]
+            turned.append(side_by_side([re * cosine + im * sine, im * cosine - re * sine]))
+        f = right(stacked(turned), m_ahead)
+        return [f[128 * i : 128 * i + 128] for i in range(len(signals))]
+
+    def inverse(spectra_in):
+        d = right(stacked([side_by_side(list(pair)) for pair in spectra_in]), m_back)
+        turned = []
+        for i in range(len(spectra_in)):
+            dr, di = d[128 * i : 128 * i + 128, :128], d[128 * i : 128 * i + 128, 128:]
+            turned.append(stacked([dr * cosine - di * sine, di * cosine + dr * sine]))
+        y = left(m_finish, side_by_side(turned))
+        return [y[:, 128 * i : 128 * i + 128] for i in range(len(spectra_in))]
+
+    def signal(slots, bq, which):
         arrived(slots.at[bq], r_z.at[8 * which + bq])
         arrived(slots.at[4 + bq], r_z.at[8 * which + 4 + bq])
-        return forward(m_signal, jnp.concatenate([slots[bq], slots[4 + bq]], axis=0))
+        return stacked([slots[bq], slots[4 + bq]])
 
     arrived(taps_all, r_txy)
-    h = forward(m_taps.at[zh], taps_all[...])
+    h = forward(m_taps.at[zh], [taps_all[...]])[0]
     hr, hi = h[:, :128], h[:, 128:]
 
     def turn(i):
@@ -250,22 +264,28 @@
                 s_bz, r_bz, device(yx, z_to, core_to),
             )
 
-    for i in range(4):
-        g = spectrum(slots_g, turn(i), 0)
-        spectra[i] = g
-        gr, gi = g[:, :128], g[:, 128:]
-        conv[pl.ds(128 * i, 128), :] = inverse(gr * hr - gi * hi, gr * hi + gi * hr)
-        spread(conv, conv_in, 128 * i, s_bxy, r_bxy.at[i])
+    for first_i in range(0, 4, 2):
+        group_i = range(first_i, first_i + 2)
+        found = forward(m_signal, [signal(slots_g, turn(i), 0) for i in group_i])
+        filtered = []
+        for i, g in zip(group_i, found):
+            spectra[i] = g
+            gr, gi = g[:, :128], g[:, 128:]
+            filtered.append((gr * hr - gi * hi, gr * hi + gi * hr))
+        for i, result in zip(group_i, inverse(filtered)):
+            conv[pl.ds(128 * i, 128), :] = result
+            spread(conv, conv_in, 128 * i, s_bxy, r_bxy.at[i])
 
     total_re = total_im = 0.0
-    for i in range(4):
-        w = spectrum(slots_w, turn(i), 1)
-        wr, wi = w[:, :128], w[:, 128:]
-        gr, gi = spectra[i, :, :128], spectra[i, :, 128:]
-        total_re = total_re + (wr * gr + wi * gi)
-        total_im = total_im + (wi * gr - wr * gi)
-
-    part[...] = inverse(total_re, total_im)
+    for first_i in range(0, 4, 4):
+        group_i = range(first_i, first_i + 4)
+        for i, w in zip(group_i, forward(m_signal, [signal(slots_w, turn(i), 1) for i in group_i])):
+            wr, wi = w[:, :128], w[:, 128:]
+            gr, gi = spectra[i, :, :128], spectra[i, :, 128:]
+            total_re = total_re + (wr * gr + wi * gi)
+            total_im = total_im + (wi * gr - wr * gi)
+
+    part[...] = inverse([(total_re, total_im)])[0]
     keeper = rem(z, 2) == core
     sibling = device(yx, z, 1 - core)
 
@@ -299,12 +319,15 @@
     arrived(grad_all.at[:, core], r_gz)
     last = remote(grad_all.at[:, core], grad_all.at[:, core], s_last, r_last, sibling)
     last.start()
+    for j in range(4):
+        block, half = pl.ds(128 * j, 128), pl.ds(128 * (j % 2), 128)
+        gated = first[block, :].astype(F32) * value[block, :].astype(F32)
+        (direct_low, direct_high)[j // 2][half, :] = gate[block, :].astype(F32) * gated
     arrived(conv_all, r_bz)
     for j in range(4):
-        block = pl.ds(128 * j, 128)
-        g = first[block, :].astype(F32) * value[block, :].astype(F32)
+        block, half = pl.ds(128 * j, 128), pl.ds(128 * (j % 2), 128)
         c = conv_all[pl.ds(j, 128, stride=4), :].T
-        out[block, :] = (gate[block, :].astype(F32) * (c + skip[...] * g)).astype(BF16)
+        (filtered_low, filtered_high)[j // 2][half, :] = gate[block, :].astype(F32) * c
 
     arrived(grad_all.at[:, 1 - core], r_last)
     flat = grad_all[...].reshape(512, 128)
@@ -337,27 +360,43 @@
         arrived(conv.at[pl.ds(0, 448)], s_gz)
 
 
+def combine(
+    filtered_low, filtered_high, direct_low, direct_high, grad_low, grad_high, skip_h, out_h, grad_h, skip, out, sems
+):
+    get = pltpu.make_async_copy(skip_h, skip, sems.at[0])
+    low = pltpu.make_async_copy(grad_low, grad_h.at[pl.ds(0, 256)], sems.at[1])
+    high = pltpu.make_async_copy(grad_high, grad_h.at[pl.ds(256, 256)], sems.at[2])
+    get.start()
+    low.start()
+    high.start()
+    get.wait()
+    out[pl.ds(0, 256), :] = (filtered_low[...] + skip[...] * direct_low[...]).astype(BF16)
+    out[pl.ds(256, 256), :] = (filtered_high[...] + skip[...] * direct_high[...]).astype(BF16)
+    put = pltpu.make_async_copy(out, out_h.at[0], sems.at[3])
+    put.start()
+    low.wait()
+    high.wait()
+    put.wait()
+
+
 def shards(first_input, value_input, gate_input, cotangent, filter_taps, skip_weight):
     constants = tables()
     vmem, hbm = pl.BlockSpec(memory_space=pltpu.VMEM), pl.BlockSpec(memory_space=pltpu.HBM)
     dma = pltpu.SemaphoreType.DMA
     square, tall, short = (pltpu.VMEM((n, 128), F32) for n in (128, 512, 64))
     operands = [
-        first_input, value_input, gate_input, cotangent, filter_taps, skip_weight[None],
+        first_input, value_input, gate_input, cotangent, filter_taps,
         *[jnp.asarray(c) for c in constants],
     ]
     long = pltpu.VMEM((512, 128), BF16)
-    out, low, high = pl.pallas_call(
+    half = jax.ShapeDtypeStruct((256, 128), F32)
+    halves_out = pl.pallas_call(
         kernel,
-        out_shape=(
-            jax.ShapeDtypeStruct((512, 128), BF16),
-            jax.ShapeDtypeStruct((256, 128), F32),
-            jax.ShapeDtypeStruct((256, 128), F32),
-        ),
-        in_specs=[hbm] * 12,
-        out_specs=(vmem, vmem, vmem),
+        out_shape=(half,) * 6,
+        in_specs=[hbm] * 11,
+        out_specs=(vmem,) * 6,
         scratch_shapes=[
-            long, long, long, long, tall, pltpu.VMEM((1, 128), F32), *[pltpu.VMEM(c.shape, c.dtype) for c in constants],
+            long, long, long, long, tall, *[pltpu.VMEM(c.shape, c.dtype) for c in constants],
             tall, tall, tall, tall, tall, tall,
             pltpu.VMEM((8, 64, 128), F32), pltpu.VMEM((8, 64, 128), F32),
             tall, short, short, square, square,
@@ -365,15 +404,26 @@
             tall, tall, tall, tall,
             square, square, square, square, square,
             pltpu.VMEM((4, 2, 64, 128), F32),
-            dma((12,)), dma, dma, dma, dma, dma, dma((8,)), dma, dma((16,)), dma, dma((4,)), dma, dma,
+            dma((11,)), dma, dma, dma, dma, dma, dma((8,)), dma, dma((16,)), dma, dma((4,)), dma, dma,
             dma, dma, dma, dma, dma, dma, dma, dma,
         ],
         compiler_params=pltpu.CompilerParams(
-            collective_id=1, has_side_effects=True, vmem_limit_bytes=56098816
+            collective_id=1, has_side_effects=True, vmem_limit_bytes=55766016
         ),
         name="hyena",
     )(*operands)
-    return out[None], jnp.concatenate([low, high], axis=0)
+    return pl.pallas_call(
+        combine,
+        out_shape=(
+            jax.ShapeDtypeStruct((1, 512, 128), BF16),
+            jax.ShapeDtypeStruct((512, 128), F32),
+        ),
+        in_specs=[vmem] * 6 + [hbm],
+        out_specs=(hbm, hbm),
+        scratch_shapes=[pltpu.VMEM((1, 128), F32), long, dma((4,))],
+        compiler_params=pltpu.CompilerParams(vmem_limit_bytes=4 * 2**20),
+        name="combine",
+    )(*halves_out, skip_weight[None])
 
 
 def solution(mesh):

time: 46.7 us -> 45.5 us (0.974)
  other arithmetic: 0.72 us -> 0 us
  local copies, waits for them, and re-layouts: 1.3 us -> 0.65 us
    concatenate x1 -> x0, other arithmetic: 0.72 us -> none  [shards(): return (out[None], jnp.concatenate([low, high], axis=0))]
    unnamed x3 -> x2, local copies, waits for them, and re-layouts: 1.3 us -> 0.65 us
    pallas_call x1 -> x2, Pallas kernels: 43.9 us -> 44.1 us  [the longest x1 43.3 us: shards(): pl.pallas_call(kernel, out_shape=(half,) * 6, in_specs=[hbm] * 11, out_sp...]
where the time goes in v4:
time: 45.5 us; the launch traced here: 45.4 us
  Pallas kernels  44.1 us (97%)
  local copies, waits for them, and re-layouts  0.65 us (1%)
  between operations  0.65 us (1%)
    pallas_call x1, Pallas kernels, shards(): pl.pallas_call(kernel, out_shape=(half,) * 6, in_specs=[hbm] * 11, out_sp...  43.3 us

profile of v4, /device:TPU:1, one launch (start us, length us, event | category | flops | bytes accessed | tf_op | source)
XLA Modules:
  0.0 45.4 jit_solution(4314002972919794252)
XLA Ops:
  0.6 43.3 %hyena.1 = (f32[256,128]{1,0:T(8,128)S(1)}, f32[256,128]{1,0:T(8,128)S(1)}, f32[256,128]{1,0:T(8,128)S(1)}, f32[256,128]{1,0:T(8,128)S(1)}, f32[256,128]{1,0:T(8,128)S(1)}, /*index=5*/f32[256,128]{1,0:T(8,128)S(1)}) custom-call(bf16[1,512,128]{2,1,0:T(8,128)(2,1)} %first_h.1, bf16[1,512,128]{2,1,0:T(8,128)(2,1)} %value_h.1, bf16[1,512,128]{2,1,0:T(8,128)(2,1)} %gate_h.1, ...), custom_call_target="tpu_custom_call" | custom-call | tf_op jit(solution)/shard_map/hyena/pallas_call | solution.py:393
  43.9 0.0 copy-start
  43.9 0.6 %copy-done = f32[128]{0:T(128)S(1)} copy-done((f32[128]{0:T(128)S(1)}, f32[128]{0:T(128)}, u32[]{:S(2)}) %copy-start) | copy-done | bytes 536
  44.6 0.8 %combine.1 = (bf16[1,512,128]{2,1,0:T(8,128)(2,1)}, f32[512,128]{1,0:T(8,128)}) custom-call(f32[256,128]{1,0:T(8,128)S(1)} %get-tuple-element.8.filtered_low, f32[256,128]{1,0:T(8,128)S(1)} %get-tuple-element.9.filtered_high, f32[256,128]{1,0:T(8,128)S(1)} %get-tuple-element.10.direct_low, f32[256,128]{1,0:T(8,128)S(1)} %get-tuple-element.11.direct_high, ...), custom_call_target="tpu_custom_call" | custom-call | tf_op jit(solution)/shard_map/combine/pallas_call | solution.py:415
Async XLA Ops:
  43.9 0.7 %copy-start = (f32[128]{0:T(128)S(1)}, f32[128]{0:T(128)}, u32[]{:S(2)}) copy-start(f32[128]{0:T(128)} %param.17) | copy-start | bytes 1540

commit v5 on v4

--- a/solution.py
+++ b/solution.py
@@ -176,8 +176,6 @@
     order = (2, 1, 3, 0)
     for dq in order:
         to_plane(tiles_g, near_g, dq, 0)
-    for c in copies[5:]:
-        c.start()
     copies[4].wait()
     for j in range(4):
         block = pl.ds(128 * j, 128)
@@ -191,9 +189,10 @@
     copies[3].wait()
     product(cot, gate, tiles_w)
     for dq in order:
+        to_column(near_g, column_g, slots_g, dq, 0)
         to_plane(tiles_w, near_w, dq, 1)
-    for dq in order:
-        to_column(near_g, column_g, slots_g, dq, 0)
+    for c in copies[5:]:
+        c.start()
 
     arrived(taps_in, r_taps)
     for j in range(4):
@@ -308,17 +307,18 @@
     def _():
         arrived(grad_in, r_gxy)
         pack(grad_in, 0, grad_pack, 0)
-        pltpu.make_async_copy(grad_pack.at[rows(64 * zh, 64)], grad_all.at[div(z, 2), core], r_gz).start()
+        pltpu.make_async_copy(grad_pack.at[rows(64 * zh, 64)], grad_all.at[div(z, 2), core], r_gz.at[div(z, 2)]).start()
         for dz in (4, 3, 5, 2, 6, 1, 7):
             zt = rem(z + dz, 8)
             remote(
-                grad_pack.at[rows(64 * div(zt, 4), 64)], grad_all.at[div(z, 2), core], s_gz, r_gz, device(yx, zt, core)
+                grad_pack.at[rows(64 * div(zt, 4), 64)], grad_all.at[div(z, 2), core], s_gz, r_gz.at[div(z, 2)], device(yx, zt, core)
             ).start()
 
     home(3)
-    arrived(grad_all.at[:, core], r_gz)
-    last = remote(grad_all.at[:, core], grad_all.at[:, core], s_last, r_last, sibling)
-    last.start()
+    for d in (0, 1, 3, 2):
+        block = grad_all.at[rem(div(z, 2) + d, 4), core]
+        arrived(block, r_gz.at[rem(div(z, 2) + d, 4)])
+        remote(block, block, s_last, r_last, sibling).start()
     for j in range(4):
         block, half = pl.ds(128 * j, 128), pl.ds(128 * (j % 2), 128)
         gated = first[block, :].astype(F32) * value[block, :].astype(F32)
@@ -335,7 +335,7 @@
     for j in range(4):
         (grad_low, grad_high)[j // 2][pl.ds(128 * (j % 2), 128), :] = taps_t[pl.ds(j, 128, stride=4), :].T
 
-    last.wait_send()
+    arrived(grad_all.at[:, core], s_last)
     arrived(taps_out, s_taps)
     arrived(taps_own.at[pl.ds(0, 120)], s_txy)
     arrived(tiles_g.at[pl.ds(0, 480)], s_xy)
@@ -405,7 +405,7 @@
             square, square, square, square, square,
             pltpu.VMEM((4, 2, 64, 128), F32),
             dma((11,)), dma, dma, dma, dma, dma, dma((8,)), dma, dma((16,)), dma, dma((4,)), dma, dma,
-            dma, dma, dma, dma, dma, dma, dma, dma,
+            dma, dma, dma, dma, dma, dma((4,)), dma, dma,
         ],
         compiler_params=pltpu.CompilerParams(
             collective_id=1, has_side_effects=True, vmem_limit_bytes=55766016

time: 45.5 us -> 45 us (0.989)
  Pallas kernels: 44.1 us -> 43.6 us
    pallas_call x1, Pallas kernels: 43.3 us -> 42.8 us  [shards(): pl.pallas_call(kernel, out_shape=(half,) * 6, in_specs=[hbm] * 11, out_sp...]
where the time goes in v5:
time: 45 us; the launch traced here: 44.9 us
  Pallas kernels  43.6 us (97%)
  local copies, waits for them, and re-layouts  0.65 us (1%)
  between operations  0.65 us (1%)
    pallas_call x1, Pallas kernels, shards(): pl.pallas_call(kernel, out_shape=(half,) * 6, in_specs=[hbm] * 11, out_sp...  42.8 us

profile of v5, /device:TPU:1, one launch (start us, length us, event | category | flops | bytes accessed | tf_op | source)
XLA Modules:
  0.0 44.9 jit_solution(5998311238083030559)
XLA Ops:
  0.6 42.8 %hyena.1 = (f32[256,128]{1,0:T(8,128)S(1)}, f32[256,128]{1,0:T(8,128)S(1)}, f32[256,128]{1,0:T(8,128)S(1)}, f32[256,128]{1,0:T(8,128)S(1)}, f32[256,128]{1,0:T(8,128)S(1)}, /*index=5*/f32[256,128]{1,0:T(8,128)S(1)}) custom-call(bf16[1,512,128]{2,1,0:T(8,128)(2,1)} %first_h.1, bf16[1,512,128]{2,1,0:T(8,128)(2,1)} %value_h.1, bf16[1,512,128]{2,1,0:T(8,128)(2,1)} %gate_h.1, ...), custom_call_target="tpu_custom_call" | custom-call | tf_op jit(solution)/shard_map/hyena/pallas_call | solution.py:393
  43.4 0.0 copy-start
  43.5 0.6 %copy-done = f32[128]{0:T(128)S(1)} copy-done((f32[128]{0:T(128)S(1)}, f32[128]{0:T(128)}, u32[]{:S(2)}) %copy-start) | copy-done | bytes 536
  44.1 0.8 %combine.1 = (bf16[1,512,128]{2,1,0:T(8,128)(2,1)}, f32[512,128]{1,0:T(8,128)}) custom-call(f32[256,128]{1,0:T(8,128)S(1)} %get-tuple-element.8.filtered_low, f32[256,128]{1,0:T(8,128)S(1)} %get-tuple-element.9.filtered_high, f32[256,128]{1,0:T(8,128)S(1)} %get-tuple-element.10.direct_low, f32[256,128]{1,0:T(8,128)S(1)} %get-tuple-element.11.direct_high, ...), custom_call_target="tpu_custom_call" | custom-call | tf_op jit(solution)/shard_map/combine/pallas_call | solution.py:415
Async XLA Ops:
  43.4 0.7 %copy-start = (f32[128]{0:T(128)S(1)}, f32[128]{0:T(128)}, u32[]{:S(2)}) copy-start(f32[128]{0:T(128)} %param.17) | copy-start | bytes 1540

commit v6 on v5

--- a/solution.py
+++ b/solution.py
@@ -139,7 +139,8 @@
             block = pl.ds(128 * j, 128)
             p = (a[block, :].astype(F32) * b[block, :].astype(F32)).T
             for zt in range(8):
-                dst[pl.ds(zt // 2 * 128 + zt % 2 * 4 + j, 16, stride=8), :] = p[16 * zt : 16 * zt + 16]
+                place = pl.ds(zt % 2 * 4 + j, 16, stride=8)
+                dst[zt // 2, place, :] = p[16 * zt : 16 * zt + 16]
 
     copies[0].wait()
     copies[1].wait()
@@ -147,13 +148,22 @@
     pl.semaphore_wait(entry, 30)
 
     def to_plane(tiles, near, dq, which):
-        base = rem(div(z, 2) + dq, 4) * 128
+        base = rem(div(z, 2) + dq, 4)
         here = rows(dq * 128 + yx * 8, 8)
         recv = r_xy.at[4 * which + dq]
-        pltpu.make_async_copy(tiles.at[rows(base + yx * 8, 8)], near.at[here], recv).start()
+        pltpu.make_async_copy(tiles.at[base, rows(yx * 8, 8)], near.at[here], recv).start()
 
         def step(there):
-            remote(tiles.at[rows(base + there * 8, 8)], near.at[here], s_xy, recv, device(there, z, core)).start()
+            remote(tiles.at[base, rows(there * 8, 8)], near.at[here], s_xy, recv, device(there, z, core)).start()
+
+        plane(step)
+
+    def all_to_plane():
+        here = near_w.at[:, rows(yx * 8, 8)]
+        pltpu.make_async_copy(tiles_w.at[:, rows(yx * 8, 8)], here, r_xy.at[4]).start()
+
+        def step(there):
+            remote(tiles_w.at[:, rows(there * 8, 8)], here, s_xy, r_xy.at[4], device(there, z, core)).start()
 
         plane(step)
 
@@ -163,8 +173,11 @@
                 dst[pl.ds(to + 64 * side + j, 16, stride=4), :] = src[pl.ds(base + 4 * side + j, 16, stride=8), :]
 
     def to_column(near, column, slots, dq, which):
-        arrived(near.at[pl.ds(dq * 128, 128)], r_xy.at[4 * which + dq])
-        pack(near, dq * 128, column, dq * 128)
+        if which:
+            pack(near.at[rem(div(z, 2) + dq, 4)], 0, column, dq * 128)
+        else:
+            arrived(near.at[pl.ds(dq * 128, 128)], r_xy.at[dq])
+            pack(near, dq * 128, column, dq * 128)
         for side in range(2):
             zt = rem(div(z, 2) + dq, 4) * 2 + side
             src, dst, recv = column.at[pl.ds(dq * 128 + side * 64, 64)], slots.at[lands], r_z.at[8 * which + lands]
@@ -173,7 +186,7 @@
             else:
                 send_or_keep(jnp.logical_and(zt == z, stays), src, dst, s_z, recv, device(yx, zt, group))
 
-    order = (2, 1, 3, 0)
+    order = (2, 3, 1, 0)
     for dq in order:
         to_plane(tiles_g, near_g, dq, 0)
     copies[4].wait()
@@ -190,7 +203,8 @@
     product(cot, gate, tiles_w)
     for dq in order:
         to_column(near_g, column_g, slots_g, dq, 0)
-        to_plane(tiles_w, near_w, dq, 1)
+        if dq == order[0]:
+            all_to_plane()
     for c in copies[5:]:
         c.start()
 
@@ -208,6 +222,7 @@
         plane(step)
 
     spread(taps_own, taps_all, 0, s_txy, r_txy)
+    arrived(near_w, r_xy.at[4])
     for dq in order:
         to_column(near_w, column_w, slots_w, dq, 1)
 
@@ -338,8 +353,8 @@
     arrived(grad_all.at[:, core], s_last)
     arrived(taps_out, s_taps)
     arrived(taps_own.at[pl.ds(0, 120)], s_txy)
-    arrived(tiles_g.at[pl.ds(0, 480)], s_xy)
-    arrived(tiles_w.at[pl.ds(0, 480)], s_xy)
+    arrived(tiles_g.at[:, pl.ds(0, 120)], s_xy)
+    arrived(tiles_w.at[:, pl.ds(0, 120)], s_xy)
     arrived(column_g.at[pl.ds(0, 448)], s_z)
     arrived(column_w.at[pl.ds(0, 448)], s_z)
     arrived(conv.at[pl.ds(0, 480)], s_bxy)
@@ -389,6 +404,7 @@
         *[jnp.asarray(c) for c in constants],
     ]
     long = pltpu.VMEM((512, 128), BF16)
+    quad = pltpu.VMEM((4, 128, 128), F32)
     half = jax.ShapeDtypeStruct((256, 128), F32)
     halves_out = pl.pallas_call(
         kernel,
@@ -397,7 +413,7 @@
         out_specs=(vmem,) * 6,
         scratch_shapes=[
             long, long, long, long, tall, *[pltpu.VMEM(c.shape, c.dtype) for c in constants],
-            tall, tall, tall, tall, tall, tall,
+            quad, quad, tall, quad, tall, tall,
             pltpu.VMEM((8, 64, 128), F32), pltpu.VMEM((8, 64, 128), F32),
             tall, short, short, square, square,
             pltpu.VMEM((4, 128, 256), F32),

time: 45 us -> 45 us (level)
  no operation moved by 1% of the time
where the time goes in v6:
time: 45 us; the launch traced here: 44.9 us
  Pallas kernels  43.6 us (97%)
  local copies, waits for them, and re-layouts  0.65 us (1%)
  between operations  0.65 us (1%)
    pallas_call x1, Pallas kernels, shards(): pl.pallas_call(kernel, out_shape=(half,) * 6, in_specs=[hbm] * 11, out_sp...  42.8 us

profile of v6, /device:TPU:1, one launch (start us, length us, event | category | flops | bytes accessed | tf_op | source)
XLA Modules:
  0.0 44.9 jit_solution(16298636854805352348)
XLA Ops:
  0.6 42.8 %hyena.1 = (f32[256,128]{1,0:T(8,128)S(1)}, f32[256,128]{1,0:T(8,128)S(1)}, f32[256,128]{1,0:T(8,128)S(1)}, f32[256,128]{1,0:T(8,128)S(1)}, f32[256,128]{1,0:T(8,128)S(1)}, /*index=5*/f32[256,128]{1,0:T(8,128)S(1)}) custom-call(bf16[1,512,128]{2,1,0:T(8,128)(2,1)} %first_h.1, bf16[1,512,128]{2,1,0:T(8,128)(2,1)} %value_h.1, bf16[1,512,128]{2,1,0:T(8,128)(2,1)} %gate_h.1, ...), custom_call_target="tpu_custom_call" | custom-call | tf_op jit(solution)/shard_map/hyena/pallas_call | solution.py:409
  43.5 0.0 copy-start
  43.5 0.6 %copy-done = f32[128]{0:T(128)S(1)} copy-done((f32[128]{0:T(128)S(1)}, f32[128]{0:T(128)}, u32[]{:S(2)}) %copy-start) | copy-done | bytes 536
  44.1 0.8 %combine.1 = (bf16[1,512,128]{2,1,0:T(8,128)(2,1)}, f32[512,128]{1,0:T(8,128)}) custom-call(f32[256,128]{1,0:T(8,128)S(1)} %get-tuple-element.8.filtered_low, f32[256,128]{1,0:T(8,128)S(1)} %get-tuple-element.9.filtered_high, f32[256,128]{1,0:T(8,128)S(1)} %get-tuple-element.10.direct_low, f32[256,128]{1,0:T(8,128)S(1)} %get-tuple-element.11.direct_high, ...), custom_call_target="tpu_custom_call" | custom-call | tf_op jit(solution)/shard_map/combine/pallas_call | solution.py:431
Async XLA Ops:
  43.5 0.7 %copy-start = (f32[128]{0:T(128)S(1)}, f32[128]{0:T(128)}, u32[]{:S(2)}) copy-start(f32[128]{0:T(128)} %param.17) | copy-start | bytes 1540
